TPU v7x, 256 devices: a whole 4x4x8 slice. The times are simulated.
256 devices in a mesh: dp: 32 (over x, z), fsdp: 8 (over y, core).
Axes of the slice: x: 4, y: 4, z: 8, core: 2. Of those that a mesh axis runs over, the one named last changes fastest.
Arguments:
- queries: bfloat16 [256, 64, 2048], P('dp'), may hold values from -6 to 6
- d_out: bfloat16 [256, 64, 2048], P('dp'), may hold values from -24 to 24
- database: bfloat16 [512, 128, 896], P('dp', 'fsdp'), may hold values from -160 to 160
- kv_weight: bfloat16 [4096, 896], P('fsdp'), may hold values from -0.1875 to 0.1875
- gain: bfloat16 [896], P('fsdp'), may hold values from 0.099609375 to 1.8984375
- nbr_owner: int32 [256, 2], replicated, may hold values from 0 to 31, all different within a row; in each aligned block of 8 rows (0 to 7, 8 to 15, ...) at most 2 rows name the same one
- nbr_row: int32 [256, 2], replicated, may hold values from 0 to 15
- nbr_count: int32 [256], P('dp'), may hold values from 1 to 2
Outputs:
- attended: bfloat16 [256, 64, 2048], P('dp', 'fsdp')
- kv_grad: float32 [4096, 896], P(('dp', 'fsdp'))
- gain_grad: float32 [896], replicated
Inputs may be any that keep to these rules, and one draw needn't show every extreme that they name: `nbr_owner`: the two owners of a stretch differ. Among the 16 entries of the stretches of one index of dp (aligned blocks of 8 stretches), no owner is named more than 2 times, a bound that some block reaches. A stretch reads its first nbr_count neighbours.
All inputs are finite; a program needn't handle non-finite values.
Results may differ from a plain program's by a relative error of at most 0.02.
Values may be sent and summed in bfloat16 or wider, within the bound.
No kernel may reach another device: no remote copies, remote signals or barrier semaphores. Data moves between devices by JAX's collectives and lax.ppermute only.
A program may use at most 128 MiB of HBM per device.

v0:
```python
import jax
import jax.numpy as jnp
from jax import lax
from jax.sharding import PartitionSpec as P

HEADS = 16


epsilon = 1e-06
clip_rms = 1.0


def rank_slots(owner_lists):
    length = owner_lists.shape[1]
    matches = owner_lists[:, :, None] == owner_lists[:, None, :]
    earlier = jnp.arange(length)[None, :] < jnp.arange(length)[:, None]
    return jnp.sum((matches & earlier[None]).astype(jnp.int32), axis=2)


def on_device(queries, d_out, database, kv_weight, gain, nbr_owner, nbr_row, nbr_count):
    groups = lax.axis_size("dp")
    shards = lax.axis_size("fsdp")
    group_index = lax.axis_index("dp")
    shard_index = lax.axis_index("fsdp")
    stretches = queries.shape[0]
    stretch_len = queries.shape[1]
    head_dim = queries.shape[2]
    slice_len = database.shape[1]
    enc_width = database.shape[2]
    entries = 2 * stretches
    capacity = max(2, (entries + groups - 1) // groups)
    head_size = head_dim // HEADS
    score_scale = head_size ** (-0.5)
    owner_lists = nbr_owner.reshape(groups, entries)
    row_lists = nbr_row.reshape(groups, entries)
    slot_rank = rank_slots(owner_lists)
    slot_ids = jnp.arange(capacity, dtype=jnp.int32)
    wanted = (owner_lists == group_index)[:, :, None] & (
        slot_rank[:, :, None] == slot_ids[None, None, :]
    )
    picked = jnp.sum(jnp.where(wanted, row_lists[:, :, None], 0), axis=1)
    outgoing = jnp.take(database, picked.reshape(-1), axis=0).reshape(
        groups, capacity, slice_len, enc_width
    )
    incoming = lax.all_to_all(outgoing, "dp", split_axis=0, concat_axis=0, tiled=True)
    my_owner = lax.dynamic_index_in_dim(owner_lists, group_index, 0, keepdims=False)
    my_rank = lax.dynamic_index_in_dim(slot_rank, group_index, 0, keepdims=False)
    fetched = jnp.take(
        incoming.reshape(groups * capacity, slice_len, enc_width),
        my_owner * capacity + my_rank,
        axis=0,
    )
    weights_full, gain_full = (
        lax.all_gather(kv_weight, "fsdp", axis=0, tiled=True),
        lax.all_gather(gain, "fsdp", axis=0, tiled=True),
    )
    raw_rows = fetched.reshape(entries * slice_len, enc_width).astype(jnp.float32)
    inv_rms = lax.rsqrt(jnp.mean(raw_rows * raw_rows, axis=1, keepdims=True) + epsilon)
    unit_rows = raw_rows * inv_rms
    normed = (unit_rows * gain_full.astype(jnp.float32)).astype(jnp.bfloat16)
    projected = lax.dot_general(
        normed, weights_full, (((1,), (1,)), ((), ())), preferred_element_type=jnp.float32
    ).astype(jnp.bfloat16)
    key_heads = projected[:, :head_dim].reshape(stretches, 2 * slice_len, HEADS, head_size)
    value_heads = projected[:, head_dim:].reshape(stretches, 2 * slice_len, HEADS, head_size)
    query_heads = queries.reshape(stretches, stretch_len, HEADS, head_size)
    grad_heads = d_out.reshape(stretches, stretch_len, HEADS, head_size)
    scores = jnp.einsum(
        "cqhd,ckhd->chqk", query_heads, key_heads, preferred_element_type=jnp.float32
    )
    neighbour = jnp.arange(2 * slice_len, dtype=jnp.int32) // slice_len
    live_mask = (neighbour[None, :] < nbr_count[:, None]).astype(jnp.float32)
    weights_exp = jnp.exp(scores * score_scale) * live_mask[:, None, None, :]
    numerator = jnp.einsum(
        "chqk,ckhd->cqhd",
        weights_exp.astype(jnp.bfloat16),
        value_heads,
        preferred_element_type=jnp.float32,
    ).reshape(stretches, stretch_len, head_dim)
    denominator = jnp.sum(weights_exp, axis=3)
    grad_dots = jnp.einsum(
        "cqhd,ckhd->chqk", grad_heads, value_heads, preferred_element_type=jnp.float32
    )
    weighted = jnp.sum(weights_exp * grad_dots, axis=3)
    rows_here = stretch_len // shards
    total_numerator, total_denominator, total_weighted = (
        lax.psum(numerator.astype(jnp.bfloat16), "fsdp").astype(jnp.float32),
        lax.psum(denominator.astype(jnp.bfloat16), "fsdp").astype(jnp.float32),
        lax.psum(weighted.astype(jnp.bfloat16), "fsdp").astype(jnp.float32),
    )
    own_rows = lax.dynamic_slice_in_dim(total_numerator, shard_index * rows_here, rows_here, 1)
    own_denominator = lax.dynamic_slice_in_dim(
        total_denominator, shard_index * rows_here, rows_here, 2
    )
    row_denominator = jnp.transpose(own_denominator, (0, 2, 1))
    attended = (
        (own_rows.reshape(stretches, rows_here, HEADS, head_size) / row_denominator[..., None])
        .reshape(stretches, rows_here, head_dim)
        .astype(jnp.bfloat16)
    )
    probabilities = weights_exp / total_denominator[..., None]
    row_delta = total_weighted / total_denominator
    score_grads = probabilities * (grad_dots - row_delta[..., None])
    grad_values = jnp.einsum(
        "chqk,cqhd->ckhd",
        probabilities.astype(jnp.bfloat16),
        grad_heads,
        preferred_element_type=jnp.float32,
    )
    grad_keys = (
        jnp.einsum(
            "chqk,cqhd->ckhd",
            score_grads.astype(jnp.bfloat16),
            query_heads,
            preferred_element_type=jnp.float32,
        )
        * score_scale
    )
    grad_proj = jnp.concatenate(
        [grad_keys.reshape(-1, head_dim), grad_values.reshape(-1, head_dim)], axis=1
    ).astype(jnp.bfloat16)
    grad_normed = jnp.dot(grad_proj, weights_full, preferred_element_type=jnp.float32)
    gain_part = jnp.sum(grad_normed * unit_rows, axis=0)
    total_rows = 2 * head_dim
    grad_shard = lax.psum_scatter(
        lax.dot_general(
            grad_proj, normed, (((0,), (0,)), ((), ())), preferred_element_type=jnp.float32
        ),
        ("dp", "fsdp"),
        scatter_dimension=0,
        tiled=True,
    )
    squares = jnp.sum(grad_shard * grad_shard)
    gain_total, square_total = lax.psum((gain_part, squares), ("dp", "fsdp"))
    entries_all = total_rows * enc_width + enc_width
    mean_square = (square_total + jnp.sum(gain_total * gain_total)) / entries_all
    factor = jnp.minimum(1.0, clip_rms / jnp.sqrt(mean_square + epsilon))
    return (attended, grad_shard * factor, gain_total * factor)


def solution(mesh):
    in_specs = (
        P("dp", None, None),
        P("dp", None, None),
        P("dp", "fsdp", None),
        P("fsdp", None),
        P("fsdp"),
        P(),
        P(),
        P("dp"),
    )
    out_specs = (P("dp", "fsdp", None), P(("dp", "fsdp"), None), P())
    return jax.shard_map(
        on_device, mesh=mesh, in_specs=in_specs, out_specs=out_specs, check_vma=False
    )
```

profile of v0, /device:TPU:48, one launch (start us, length us, event | category | flops | bytes accessed | tf_op | source)
XLA Modules:
  0.0 1567.4 jit_solution(14491082449153848395)
XLA Ops:
  7.2 0.7 all-gather.2.cloned.1.call-update
  7.9 0.8 copy.49
  9.0 0.8 copy.54
  10.5 2.0 gather_fusion
  12.5 3.0 broadcast_select_fusion
  15.5 11.4 all-to-all-start
  27.0 0.6 dynamic-slice
  28.5 11.0 all-reduce
  40.0 30.9 %all-to-all-done = bf16[32,2,16,896]{3,2,1,0:T(8,128)(2,1)} async-done(((bf16[32,2,16,896]{3,2,1,0:T(8,128)(2,1)}), bf16[32,2,16,896]{3,2,1,0:T(8,128)(2,1)}, u32[]{:S(2)}, u32[]{:S(2)}) %all-to-all-start) | async-done | bytes 1835040 | tf_op jit(solution)/shard_map/all_to_all | solution.py:45
  70.9 2.1 gather_fusion.1
  73.5 5.6 convolution_convert_fusion
  79.8 1.1 copy-done.6
  80.9 1.2 exponential_multiply_fusion
  82.2 2.7 fusion.8
  84.8 20.7 %all-reduce.2 = (bf16[8,16,64]{2,1,0:T(8,128)(2,1)S(1)}, bf16[8,16,64]{2,1,0:T(8,128)(2,1)S(1)}) all-reduce(bf16[8,16,64]{2,1,0:T(8,128)(2,1)S(1)} %get-tuple-element.4, bf16[8,16,64]{2,1,0:T(8,128)(2,1)S(1)} %get-tuple-element.3), channel_id=1, replica_groups=mesh['dp'=32,'fsdp'=8] {'fsdp'}, use_global_device_ids=true, to_apply=%region_5.6 | all-reduce | flops 16384 | bytes 65536 | tf_op jit(solution)/shard_map/psum | solution.py:88
  105.6 2.4 fusion.22
  108.5 1.3 copy-done.2
  109.7 0.7 fusion.25
  111.3 1.4 copy-done.4
  112.7 7.7 fusion.36
  120.5 2.3 convert_bitcast_fusion
  122.8 1.9 copy.114
  124.8 0.9 copy-done.10
  125.7 6.1 fusion.28
  131.8 1242.8 %reduce-scatter.2.cloned.1.call-done = f32[16,896]{1,0:T(8,128)} async-done(((f32[4096,896]{1,0:T(8,128)}), f32[16,896]{1,0:T(8,128)}) %reduce-scatter.2.cloned.1.call-update) | async-done | bytes 57360 | tf_op jit(solution)/shard_map/reduce_scatter | solution.py:125
  1374.6 1.4 multiply_reduce_fusion.1
  1376.0 99.8 %all-reduce.5.cloned.1.call-done = bf16[8,64,2048]{2,1,0:T(8,128)(2,1)} async-done(((bf16[8,64,2048]{2,1,0:T(8,128)(2,1)}), bf16[8,64,2048]{2,1,0:T(8,128)(2,1)}) %all-reduce.5.cloned.1.call-update) | async-done | bytes 2097168 | tf_op jit(solution)/shard_map/psum | solution.py:87
  1475.8 1.9 fusion.35
  1477.7 79.2 %all-reduce.1 = (f32[]{:T(128)}, f32[896]{0:T(1024)S(1)}) all-reduce(f32[]{:T(128)} %multiply_reduce_fusion.1, f32[896]{0:T(1024)S(1)} %fusion.28), channel_id=1, replica_groups=mesh['dp'=32,'fsdp'=8] {'dp','fsdp'}, use_global_device_ids=true, to_apply=%region_10.11 | all-reduce | flops 897 | bytes 7176 | tf_op jit(solution)/shard_map/psum | solution.py:134
  1556.9 0.6 multiply_reduce_fusion.2
  1558.8 0.6 broadcast_multiply_fusion.1
  1559.4 1.4 broadcast_multiply_fusion
  (70 shorter events, 4.3 us)
Async XLA Ops:
  7.2 75.0 %copy-start = (bf16[8,64,2048]{2,1,0:T(8,128)(2,1)S(1)}, bf16[8,64,2048]{2,1,0:T(8,128)(2,1)}, u32[]{:S(2)}) copy-start(bf16[8,64,2048]{2,1,0:T(8,128)(2,1)} %param.9) | copy-start | bytes 6291460
  7.2 3.3 copy-start.3
  7.2 66.3 %all-gather.2.cloned.1.call-start = ((), (), s32[]{:S(2)}) async-start(), calls=%async_computation.2 | async-start | bytes 8257536 | tf_op jit(solution)/shard_map/all_gather | solution.py:54
  15.5 11.4 copy-start.13
  15.5 12.7 copy-start.12
  15.5 24.4 %copy-start.11 = (s32[8]{0:T(128)S(1)}, s32[8]{0:T(128)}, u32[]{:S(2)}) copy-start(s32[8]{0:T(128)} %param.15) | copy-start | bytes 100
  15.5 55.4 %all-to-all-start = ((bf16[32,2,16,896]{3,2,1,0:T(8,128)(2,1)}), bf16[32,2,16,896]{3,2,1,0:T(8,128)(2,1)}, u32[]{:S(2)}, u32[]{:S(2)}) async-start(bf16[32,2,16,896]{3,2,1,0:T(8,128)(2,1)} %broadcast_select_fusion), calls=%async_computation | async-start | bytes 3670016 | tf_op jit(solution)/shard_map/all_to_all | solution.py:45
  26.9 1347.7 %reduce-scatter.2.cloned.1.call-start = ((), (), s32[]{:S(2)}) async-start(), calls=%async_computation.4 | async-start | bytes 14737408 | tf_op jit(solution)/shard_map/reduce_scatter | solution.py:125
  73.5 5.7 copy-start.8
  79.3 1.6 copy-start.6
  82.1 2.7 copy-start.1
  105.6 2.9 copy-start.5
  105.6 2.9 copy-start.7
  108.0 1.7 copy-start.2
  110.8 1.9 copy-start.9
  111.3 1.4 copy-start.4
  120.4 1355.4 %all-reduce.5.cloned.1.call-start = ((), (), s32[]{:S(2)}) async-start(), calls=%async_computation.3 | async-start | bytes 4194304 | tf_op jit(solution)/shard_map/psum | solution.py:87
  124.7 1.0 copy-start.10
Sparse Core Ops, SparseCore 0:
  9.9 49.2 all-gather.1
  120.5 1254.0 reduce-scatter.1
  1377.1 98.6 all-reduce.4
where the time goes:
time: 1570 us
  waiting for transfers between devices  1370 us (87%)
  blocking collectives  111 us (7%)
  matrix products  28.7 us (2%)
  local copies, waits for them, and re-layouts  16.1 us (1%)
  between operations  16.1 us (1%)
    reduce_scatter x1, waiting for transfers between devices, on_device(): lax.psum_scatter(lax.dot_general(grad_proj, normed, (((0,), (0,)), ((), (...  1240 us
    psum x1, waiting for transfers between devices, on_device(): lax.psum(numerator.astype(jnp.bfloat16), 'fsdp').astype(jnp.float32)  99.8 us
    psum x1, blocking collectives, on_device(): gain_total, square_total = lax.psum((gain_part, squares), ('dp', 'fsdp'))  79.2 us
  transfers between devices with their start and end apart: 4, of which 3 were waited for; matrix products, arithmetic and copies ran while one was open for 1% of the time, Pallas kernels for 0%

commit v1 on v0

v1 whole, which is shorter than its diff:
```python
import jax
import jax.numpy as jnp
from jax import lax
from jax.experimental import pallas as pl
from jax.experimental.pallas import tpu as pltpu
from jax.sharding import PartitionSpec as P

HEADS = 16
HEAD = 128
epsilon = 1e-06
clip_rms = 1.0
f32 = jnp.float32
bf16 = jnp.bfloat16


def dot(a, b, ca, cb):
    return lax.dot_general(a, b, (((ca,), (cb,)), ((), ())), preferred_element_type=f32)


def main_kernel(me_ref, count_ref, x_ref, w_ref, gain_ref, q_ref, do_ref, att_ref, out_ref, acc_ref):
    c = pl.program_id(0)
    width = x_ref.shape[-1]
    keys = x_ref.shape[0] * x_ref.shape[1] * x_ref.shape[2]
    scale = HEAD ** (-0.5)
    gain = gain_ref[...].astype(f32)
    x = x_ref[...].reshape(keys, width).astype(f32)
    inv = lax.rsqrt(jnp.mean(x * x, axis=1, keepdims=True) + epsilon)
    normed = ((x * inv) * gain).astype(bf16)
    proj = dot(w_ref[...], normed, 1, 1).astype(bf16)
    lane = lax.broadcasted_iota(jnp.int32, (1, keys), 1)
    live = (((lane // 16) % 2) < count_ref[c]).astype(f32)
    grads = [None] * 4
    for a in range(2):
        cols = slice(a * HEAD, (a + 1) * HEAD)
        key_t = proj[a * HEAD : (a + 1) * HEAD]
        val_t = proj[(2 + a) * HEAD : (3 + a) * HEAD]
        q = q_ref[0, :, cols]
        do = do_ref[0, :, cols]
        weights = jnp.exp(dot(q, key_t, 1, 0) * scale) * live
        inv_den = 1.0 / jnp.sum(weights, axis=1, keepdims=True)
        numerator = dot(weights.astype(bf16), val_t, 1, 1)
        dots = dot(do, val_t, 1, 0)
        delta = jnp.sum(weights * dots, axis=1, keepdims=True) * inv_den
        att_ref[0, :, cols] = (numerator * inv_den).astype(bf16)
        prob = weights * inv_den
        score_grad = prob * (dots - delta)
        grads[a] = dot(q, score_grad.astype(bf16), 0, 0) * scale
        grads[2 + a] = dot(do, prob.astype(bf16), 0, 0)
    grad_t = jnp.concatenate(grads, axis=0).astype(bf16)
    part = dot(grad_t, normed, 1, 0)

    @pl.when(c == 0)
    def _():
        acc_ref[...] = part

    @pl.when(c > 0)
    def _():
        acc_ref[...] += part

    @pl.when(c == pl.num_programs(0) - 1)
    def _():
        blocks = out_ref.shape[0]
        total = acc_ref[...]
        out_ref[:, :, :width] = total.reshape(blocks, 16, width).astype(bf16)
        gain_part = jnp.sum(total * w_ref[...].astype(f32), axis=0, keepdims=True) / gain
        row = lax.broadcasted_iota(jnp.int32, (16, 128), 0)
        out_ref[:, :, width:] = jnp.zeros((blocks, 16, 128), bf16)
        for t in range(width // 128):
            piece = jnp.broadcast_to(gain_part[:, t * 128 : (t + 1) * 128], (16, 128))
            high = piece.astype(bf16).astype(f32)
            tile = jnp.where(row == 0, high, jnp.where(row == 1, piece - high, 0.0)).astype(bf16)
            for quarter in range(4):
                out_ref[4 * t + quarter, :, width:] = tile


def main_call(me, count, tokens, weights, gain, queries, d_out):
    shards, entries, per, width = tokens.shape
    stretches, length, _ = queries.shape
    rows = weights.shape[0]
    blocks = rows // 16
    pair = 2 * HEAD
    grid_spec = pltpu.PrefetchScalarGridSpec(
        num_scalar_prefetch=2,
        grid=(stretches,),
        in_specs=[
            pl.BlockSpec((shards, 2, per, width), lambda c, me, n: (0, c, 0, 0)),
            pl.BlockSpec((rows, width), lambda c, me, n: (0, 0)),
            pl.BlockSpec((1, width), lambda c, me, n: (0, 0)),
            pl.BlockSpec((1, length, pair), lambda c, me, n: (c, 0, me[1])),
            pl.BlockSpec((1, length, pair), lambda c, me, n: (c, 0, me[1])),
        ],
        out_specs=[
            pl.BlockSpec((1, length, pair), lambda c, me, n: (c, 0, 0)),
            pl.BlockSpec((blocks, 16, width + 128), lambda c, me, n: (0, 0, 0)),
        ],
        scratch_shapes=[pltpu.VMEM((rows, width), f32)],
    )
    return pl.pallas_call(
        main_kernel,
        grid_spec=grid_spec,
        out_shape=[
            jax.ShapeDtypeStruct((stretches, length, pair), bf16),
            jax.ShapeDtypeStruct((blocks, 16, width + 128), bf16),
        ],
        compiler_params=pltpu.CompilerParams(vmem_limit_bytes=40 * 1024 * 1024),
        cost_estimate=pl.CostEstimate(flops=4_200_000_000, bytes_accessed=8_000_000, transcendentals=262144),
        name="attend",
    )(me, count, tokens, weights, gain, queries, d_out)


def reduce_kernel(me_ref, in_ref, red_ref, pay_ref):
    width = red_ref.shape[1]
    blocks = in_ref.shape[0]
    total = in_ref[0].astype(f32)
    for i in range(1, blocks):
        total = total + in_ref[i].astype(f32)
    red = total[:, :width]
    red_ref[...] = red
    squares = jnp.sum(jnp.sum(red * red, axis=1, keepdims=True), axis=0, keepdims=True)
    gain = total[0:1, width:] + total[1:2, width:]
    quarter = me_ref[0] % 4
    lane = lax.broadcasted_iota(jnp.int32, (1, 128), 1)
    gain = jnp.where(lane // 32 == quarter, gain, 0.0)
    pay = jnp.where(lane == ((quarter + 1) % 4) * 32, squares, gain)
    pay_ref[...] = jnp.broadcast_to(pay[None], pay_ref.shape)


def final_kernel(pay_ref, red_ref, grad_ref, gain_ref):
    blocks = 32
    pay = pay_ref[...].reshape(blocks, 8, 128)
    rows = jnp.sum(pay, axis=1)
    row = lax.broadcasted_iota(jnp.int32, (blocks, 128), 0)
    lane = lax.broadcasted_iota(jnp.int32, (blocks, 128), 1)
    gains = jnp.where((lane // 32 == row % 4) & (row < 28), rows, 0.0)
    gains = jnp.sum(gains.reshape(8, 4, 128), axis=1)
    squares = jnp.where(lane == ((row + 1) % 4) * 32, rows, 0.0)
    total = jnp.sum(jnp.sum(squares, axis=1, keepdims=True), axis=0, keepdims=True)
    total = total + jnp.sum(jnp.sum(gains * gains, axis=1, keepdims=True), axis=0, keepdims=True)
    count = 4096 * 896 + 896
    factor = jnp.minimum(1.0, clip_rms * lax.rsqrt(total / count + epsilon))
    grad_ref[...] = red_ref[...] * factor
    gain_ref[...] = gains * factor


def on_device(queries, d_out, database, kv_weight, gain, nbr_owner, nbr_row, nbr_count):
    groups = lax.axis_size("dp")
    shards = lax.axis_size("fsdp")
    group = lax.axis_index("dp")
    shard = lax.axis_index("fsdp")
    me = jnp.stack([group, shard]).astype(jnp.int32)
    stretches, length, head_dim = queries.shape
    per, width = database.shape[1:]
    entries = 2 * stretches
    capacity = 2
    owners = nbr_owner.reshape(groups, entries)
    rows = nbr_row.reshape(groups, entries)
    same = owners[:, :, None] == owners[:, None, :]
    earlier = jnp.arange(entries)[None, :] < jnp.arange(entries)[:, None]
    rank = jnp.sum((same & earlier[None]).astype(jnp.int32), axis=2)
    slots = jnp.arange(capacity, dtype=jnp.int32)
    wanted = (owners == group)[:, :, None] & (rank[:, :, None] == slots[None, None, :])
    picked = jnp.sum(jnp.where(wanted, rows[:, :, None], 0), axis=1)
    outgoing = jnp.take(database, picked.reshape(-1), axis=0, mode="clip")
    incoming = lax.all_to_all(
        outgoing.reshape(groups, capacity, per, width), "dp", split_axis=0, concat_axis=0, tiled=True
    )
    my_owner = lax.dynamic_index_in_dim(owners, group, 0, keepdims=False)
    my_rank = lax.dynamic_index_in_dim(rank, group, 0, keepdims=False)
    fetched = jnp.take(
        incoming.reshape(groups * capacity, per, width), my_owner * capacity + my_rank, axis=0, mode="clip"
    )
    half = kv_weight.shape[0] // 2
    high = shard >= shards // 2
    first, second = kv_weight[:half], kv_weight[half:]
    low_half = shards // 2
    pairs_a = [(i, 2 * i) for i in range(low_half)] + [(i + low_half, 2 * i + 1) for i in range(low_half)]
    pairs_b = [(i, 2 * i + 1) for i in range(low_half)] + [(i + low_half, 2 * i) for i in range(low_half)]
    got_a = lax.ppermute(jnp.where(high, second, first), "fsdp", pairs_a)
    got_b = lax.ppermute(jnp.where(high, first, second), "fsdp", pairs_b)
    odd = shard % 2 == 1
    weights = jnp.concatenate([jnp.where(odd, got_b, got_a), jnp.where(odd, got_a, got_b)], axis=0)
    gain_full = lax.all_gather(gain, "fsdp", axis=0, tiled=True).reshape(1, width)
    tokens = lax.all_gather(fetched, "fsdp", axis=0, tiled=False)
    att, blocks = main_call(me, nbr_count, tokens, weights, gain_full, queries, d_out)
    rows_here = length // shards
    att = att.reshape(stretches, shards, rows_here, 2 * HEAD).transpose(1, 0, 2, 3)
    att = lax.all_to_all(att, "fsdp", split_axis=0, concat_axis=0, tiled=True)
    attended = att.transpose(1, 2, 0, 3).reshape(stretches, rows_here, head_dim)
    blocks = lax.all_to_all(blocks, "dp", split_axis=0, concat_axis=0, tiled=True)
    reduced, payload = pl.pallas_call(
        reduce_kernel,
        in_specs=[pl.BlockSpec(memory_space=pltpu.SMEM), pl.BlockSpec(memory_space=pltpu.VMEM)],
        out_specs=[pl.BlockSpec(memory_space=pltpu.VMEM)] * 2,
        out_shape=[
            jax.ShapeDtypeStruct((16, width), f32),
            jax.ShapeDtypeStruct((groups * shards, 1, 128), f32),
        ],
        compiler_params=pltpu.CompilerParams(vmem_limit_bytes=16 * 1024 * 1024),
        name="reduce",
    )(me, blocks)
    pairs = []
    for p in range(groups):
        kv, odd_head, piece = p // 16, (p // 8) % 2, p % 8
        for s in range(shards):
            pairs.append((p * shards + s, (kv * 16 + 2 * s + odd_head) * shards + piece))
    moved = lax.ppermute(reduced, ("dp", "fsdp"), pairs)
    payload = lax.all_to_all(payload, ("dp", "fsdp"), split_axis=0, concat_axis=0, tiled=True)
    kv_grad, gain_grad = pl.pallas_call(
        final_kernel,
        out_shape=[
            jax.ShapeDtypeStruct((16, width), f32),
            jax.ShapeDtypeStruct((8, 128), f32),
        ],
        name="finish",
    )(payload, moved)
    return attended, kv_grad, gain_grad[: width // 128].reshape(width)


def solution(mesh):
    in_specs = (
        P("dp", None, None),
        P("dp", None, None),
        P("dp", "fsdp", None),
        P("fsdp", None),
        P("fsdp"),
        P(),
        P(),
        P("dp"),
    )
    out_specs = (P("dp", "fsdp", None), P(("dp", "fsdp"), None), P())
    return jax.shard_map(
        on_device, mesh=mesh, in_specs=in_specs, out_specs=out_specs, check_vma=False
    )
```

time: 1570 us -> 209 us (0.13)
  waiting for transfers between devices: 1370 us -> 93.5 us
  blocking collectives: 111 us -> 18.4 us
  matrix products: 28.7 us -> 0 us
  starting transfers between devices: 11.5 us -> 39.8 us
  Pallas kernels: 0 us -> 24.3 us
    reduce_scatter x1 -> x0, waiting for transfers between devices: 1240 us -> none  [on_device(): lax.psum_scatter(lax.dot_general(grad_proj, normed, (((0,), (0,)), ((), (...]
    psum x2 -> x0, blocking collectives: 100 us -> none  [the longest x1 79.2 us: on_device(): gain_total, square_total = lax.psum((gain_part, squares), ('dp', 'fsdp'))]
    psum x1 -> x0, waiting for transfers between devices: 99.8 us -> none  [on_device(): lax.psum(numerator.astype(jnp.bfloat16), 'fsdp').astype(jnp.float32)]
    all_to_all x1 -> x4, waiting for transfers between devices: 30.9 us -> 74.6 us  [the longest x1 43.7 us: on_device(): lax.all_to_all(outgoing.reshape(groups, capacity, per, width), 'dp', spli...]
    dot_general x8 -> x0, matrix products: 28.7 us -> none  [the longest x1 7.69 us: on_device(): lax.dot_general(grad_proj, normed, (((0,), (0,)), ((), ())), preferred_el...]
    pallas_call x0 -> x3, Pallas kernels: none -> 24.3 us  [the longest x1 21.1 us: main_call(): pl.pallas_call(main_kernel, grid_spec=grid_spec, out_shape=[jax.ShapeDtyp...]
    all_to_all x1 -> x4, starting transfers between devices: 11.4 us -> 34.2 us  [the longest x1 11.3 us: on_device(): lax.all_to_all(outgoing.reshape(groups, capacity, per, width), 'dp', spli...]
  transfers between devices with their start and end apart: 4 -> 8, of which waited for: 3 -> 5; matrix products, arithmetic and copies ran while one was open for 1% -> 2% of each run, Pallas kernels for 0% -> 1%
where the time goes in v1:
time: 209 us; the launch traced here: 208 us
  waiting for transfers between devices  93.5 us (45%)
  starting transfers between devices  39.8 us (19%)
  Pallas kernels  24.3 us (12%)
  blocking collectives  18.4 us (9%)
  local copies, waits for them, and re-layouts  15.7 us (8%)
  between operations  14.9 us (7%)
    all_to_all x1, waiting for transfers between devices, on_device(): lax.all_to_all(outgoing.reshape(groups, capacity, per, width), 'dp', spli...  43.7 us
    all_to_all x1, waiting for transfers between devices, on_device(): lax.all_to_all(blocks, 'dp', split_axis=0, concat_axis=0, tiled=True)  28 us
    pallas_call x1, Pallas kernels, main_call(): pl.pallas_call(main_kernel, grid_spec=grid_spec, out_shape=[jax.ShapeDtyp...  21.1 us
    unnamed x1, blocking collectives  18.4 us
    ppermute x1, waiting for transfers between devices, on_device(): moved = lax.ppermute(reduced, ('dp', 'fsdp'), pairs)  11.8 us
    all_to_all x1, starting transfers between devices, on_device(): lax.all_to_all(outgoing.reshape(groups, capacity, per, width), 'dp', spli...  11.3 us
    all_to_all x1, starting transfers between devices, on_device(): lax.all_to_all(payload, ('dp', 'fsdp'), split_axis=0, concat_axis=0, tile...  9.31 us
    unnamed x25, local copies, waits for them, and re-layouts  9.02 us
  transfers between devices with their start and end apart: 8, of which 5 were waited for; matrix products, arithmetic and copies ran while one was open for 2% of the time, Pallas kernels for 1%

profile of v1, /device:TPU:48, one launch (start us, length us, event | category | flops | bytes accessed | tf_op | source)
XLA Modules:
  0.0 208.1 jit_solution(4052788888858196362)
XLA Ops:
  7.2 0.9 copy.30
  8.3 0.8 copy.34
  9.7 2.0 gather_fusion
  11.7 11.3 %all-to-all-start = ((bf16[32,2,16,896]{3,2,1,0:T(8,128)(2,1)}), bf16[32,2,16,896]{3,2,1,0:T(8,128)(2,1)S(1)}, u32[]{:S(2)}, u32[]{:S(2)}) async-start(bf16[32,2,16,896]{3,2,1,0:T(8,128)(2,1)} %bitcast.2), calls=%async_computation | async-start | bytes 3670016 | tf_op jit(solution)/shard_map/all_to_all | solution.py:164
  23.1 0.2 add_reduce_fusion
  23.3 43.7 %all-to-all-done = bf16[32,2,16,896]{3,2,1,0:T(8,128)(2,1)S(1)} async-done(((bf16[32,2,16,896]{3,2,1,0:T(8,128)(2,1)}), bf16[32,2,16,896]{3,2,1,0:T(8,128)(2,1)S(1)}, u32[]{:S(2)}, u32[]{:S(2)}) %all-to-all-start) | async-done | bytes 1835040 | tf_op jit(solution)/shard_map/all_to_all | solution.py:164
  67.0 1.4 gather_fusion.1
  68.4 0.9 broadcast_select_fusion.1
  69.3 0.3 collective-permute-start
  69.6 2.4 %collective-permute-start.1 = (bf16[256,896]{1,0:T(8,128)(2,1)S(1)}, bf16[256,896]{1,0:T(8,128)(2,1)S(1)}, u32[]{:S(2)}, u32[]{:S(2)}) collective-permute-start(bf16[256,896]{1,0:T(8,128)(2,1)S(1)} %get-tuple-element.18), channel_id=1, source_target_pairs={{0,0},{1,2},{2,4},{3,6},{4,1},{5,3},{6,5},{7,7},{8,8},{9,10},{10,1... | collective-permute-start | bytes 1376264 | tf_op jit(solution)/shard_map/ppermute | solution.py:178
  72.0 0.6 dynamic-slice
  73.3 0.2 dynamic-update-slice
  73.5 18.4 %all-reduce = bf16[896]{0:T(1024)(128)(2,1)S(1)} all-reduce(bf16[896]{0:T(1024)(128)(2,1)S(1)} %dynamic-update-slice), channel_id=1, replica_groups=mesh['dp'=32,'fsdp'=8] {'fsdp'}, use_global_device_ids=true, to_apply=%add | all-reduce | flops 896 | bytes 3584
  92.2 7.1 %all-gather.3.cloned.1.call-done = bf16[128,16,896]{2,1,0:T(8,128)(2,1)} async-done(((bf16[16,16,896]{2,1,0:T(8,128)(2,1)}), bf16[128,16,896]{2,1,0:T(8,128)(2,1)}) %all-gather.3.cloned.1.call-update) | async-done | bytes 3670032 | tf_op jit(solution)/shard_map/all_gather | solution.py:183
  99.3 2.0 copy-done.1
  101.4 1.6 copy-done.2
  102.9 1.6 copy-done.3
  104.5 21.1 %attend.1 = (bf16[8,64,256]{2,1,0:T(8,128)(2,1)S(1)}, bf16[32,16,1024]{2,1,0:T(8,128)(2,1)}) custom-call(s32[2]{0:T(128)S(1)} %pad_add_fusion.me_ref, s32[8]{0:T(128)S(1)} %copy-done.4, bf16[8,16,16,896]{3,2,1,0:T(8,128)(2,1)S(1)} %bitcast.16, bf16[512,896]{1,0:T(8,128)(2,1)S(1)} %pad_maximum_fusion.w_ref, bf16[1,896]{1,0:T(2,128)(2,1)S(1)} %reshape.76.gain_ref, ...), custom_call_target="tpu_custom_call" | custom-call | flops 4200000000 | bytes 8000000 | tf_op jit(solution)/shard_map/attend/pallas_call | solution.py:98
  125.6 8.3 %all-to-all-start.2 = ((bf16[32,16,1024]{2,1,0:T(8,128)(2,1)}), bf16[32,16,1024]{2,1,0:T(8,128)(2,1)S(1)}, u32[]{:S(2)}, u32[]{:S(2)}) async-start(bf16[32,16,1024]{2,1,0:T(8,128)(2,1)} %get-tuple-element.10), calls=%async_computation.2 | async-start | bytes 2097152 | tf_op jit(solution)/shard_map/all_to_all | solution.py:189
  133.9 0.7 copy_bitcast_fusion
  134.6 28.0 %all-to-all-done.2.in_ref = bf16[32,16,1024]{2,1,0:T(8,128)(2,1)S(1)} async-done(((bf16[32,16,1024]{2,1,0:T(8,128)(2,1)}), bf16[32,16,1024]{2,1,0:T(8,128)(2,1)S(1)}, u32[]{:S(2)}, u32[]{:S(2)}) %all-to-all-start.2) | async-done | bytes 1048608 | tf_op jit(solution)/shard_map/all_to_all | solution.py:189
  162.7 5.2 %all-to-all-start.1 = ((bf16[8,8,8,256]{3,2,1,0:T(8,128)(2,1)}), bf16[8,8,8,256]{3,2,1,0:T(8,128)(2,1)S(1)}, u32[]{:S(2)}, u32[]{:S(2)}) async-start(bf16[8,8,8,256]{3,2,1,0:T(8,128)(2,1)} %copy_bitcast_fusion), calls=%async_computation.1 | async-start | bytes 524288 | tf_op jit(solution)/shard_map/all_to_all | solution.py:187
  167.9 1.5 reduce.3
  169.4 2.9 %all-to-all-done.1 = bf16[8,8,8,256]{3,2,1,0:T(8,128)(2,1)S(1)} async-done(((bf16[8,8,8,256]{3,2,1,0:T(8,128)(2,1)}), bf16[8,8,8,256]{3,2,1,0:T(8,128)(2,1)S(1)}, u32[]{:S(2)}, u32[]{:S(2)}) %all-to-all-start.1) | async-done | bytes 262176 | tf_op jit(solution)/shard_map/all_to_all | solution.py:187
  172.2 9.3 %all-to-all-start.3 = ((f32[256,1,128]{2,1,0:T(1,128)}), f32[256,1,128]{2,1,0:T(1,128)S(1)}, u32[]{:S(2)}, u32[]{:S(2)}) async-start(f32[256,1,128]{2,1,0:T(1,128)} %get-tuple-element.11), calls=%async_computation.3 | async-start | bytes 262144 | tf_op jit(solution)/shard_map/all_to_all | solution.py:207
  181.6 2.9 %collective-permute-start.2 = (f32[16,896]{1,0:T(8,128)S(1)}, f32[16,896]{1,0:T(8,128)S(1)}, u32[]{:S(2)}, u32[]{:S(2)}) collective-permute-start(f32[16,896]{1,0:T(8,128)S(1)} %get-tuple-element.12), channel_id=1, source_target_pairs={{0,0},{1,16},{2,32},{3,48},{4,64},{5,80},{6,96},{7,112},{8,1},{9,1... | collective-permute-start | bytes 172040 | tf_op jit(solution)/shard_map/ppermute | solution.py:206
  184.4 0.7 copy.40
  185.1 11.8 %collective-permute-done.2.red_ref = f32[16,896]{1,0:T(8,128)S(1)} collective-permute-done((f32[16,896]{1,0:T(8,128)S(1)}, f32[16,896]{1,0:T(8,128)S(1)}, u32[]{:S(2)}, u32[]{:S(2)}) %collective-permute-start.2) | collective-permute-done | bytes 57376 | tf_op jit(solution)/shard_map/ppermute | solution.py:206
  197.0 0.6 copy-done.7
  197.6 0.7 copy-done.6
  198.2 1.7 finish.1
  200.0 1.3 slice_bitcast_fusion
  (38 shorter events, 1.2 us)
Async XLA Ops:
  7.2 2.5 %copy-start = (bf16[16,16,896]{2,1,0:T(8,128)(2,1)S(1)}, bf16[16,16,896]{2,1,0:T(8,128)(2,1)}, u32[]{:S(2)}) copy-start(bf16[16,16,896]{2,1,0:T(8,128)(2,1)} %param.10) | copy-start | bytes 1376260
  11.7 56.7 %copy-start.5 = (bf16[512,896]{1,0:T(8,128)(2,1)S(1)}, bf16[512,896]{1,0:T(8,128)(2,1)}, u32[]{:S(2)}) copy-start(bf16[512,896]{1,0:T(8,128)(2,1)} %param.11) | copy-start | bytes 2752516
  11.7 55.3 %all-to-all-start = ((bf16[32,2,16,896]{3,2,1,0:T(8,128)(2,1)}), bf16[32,2,16,896]{3,2,1,0:T(8,128)(2,1)S(1)}, u32[]{:S(2)}, u32[]{:S(2)}) async-start(bf16[32,2,16,896]{3,2,1,0:T(8,128)(2,1)} %bitcast.2), calls=%async_computation | async-start | bytes 3670016 | tf_op jit(solution)/shard_map/all_to_all | solution.py:164
  23.0 48.9 %copy-start.9 = (u32[256]{0:T(256)S(1)}, u32[256]{0:T(256)}, u32[]{:S(2)}) copy-start(u32[256]{0:T(256)} %constant.40) | copy-start | bytes 3076
  23.1 50.2 %copy-start.8 = (bf16[112]{0:T(256)(128)(2,1)S(1)}, bf16[112]{0:T(256)(128)(2,1)}, u32[]{:S(2)}) copy-start(bf16[112]{0:T(256)(128)(2,1)} %param.12) | copy-start | bytes 676
  23.1 76.2 %all-gather.3.cloned.1.call-start = ((), (), s32[]{:S(2)}) async-start(), calls=%async_computation.4 | async-start | bytes 4128768 | tf_op jit(solution)/shard_map/all_gather | solution.py:183
  69.3 22.7 %collective-permute-start = (bf16[256,896]{1,0:T(8,128)(2,1)}, bf16[256,896]{1,0:T(8,128)(2,1)S(1)}, u32[]{:S(2)}, u32[]{:S(2)}) collective-permute-start(bf16[256,896]{1,0:T(8,128)(2,1)} %get-tuple-element.17), channel_id=1, source_target_pairs={{0,1},{1,3},{2,5},{3,7},{4,0},{5,2},{6,4},{7,6},{8,9},{9,11},{10,1... | collective-permute-start | bytes 1376264 | tf_op jit(solution)/shard_map/ppermute | solution.py:179
  69.6 22.4 %collective-permute-start.1 = (bf16[256,896]{1,0:T(8,128)(2,1)S(1)}, bf16[256,896]{1,0:T(8,128)(2,1)S(1)}, u32[]{:S(2)}, u32[]{:S(2)}) collective-permute-start(bf16[256,896]{1,0:T(8,128)(2,1)S(1)} %get-tuple-element.18), channel_id=1, source_target_pairs={{0,0},{1,2},{2,4},{3,6},{4,1},{5,3},{6,5},{7,7},{8,8},{9,10},{10,1... | collective-permute-start | bytes 1376264 | tf_op jit(solution)/shard_map/ppermute | solution.py:178
  92.0 7.4 %copy-start.4 = (s32[8]{0:T(128)S(1)}, s32[8]{0:T(128)}, u32[]{:S(2)}) copy-start(s32[8]{0:T(128)} %count_ref.1) | copy-start | bytes 100
  99.3 2.0 copy-start.1
  101.4 1.6 copy-start.2
  102.9 1.6 copy-start.3
  125.6 37.1 %all-to-all-start.2 = ((bf16[32,16,1024]{2,1,0:T(8,128)(2,1)}), bf16[32,16,1024]{2,1,0:T(8,128)(2,1)S(1)}, u32[]{:S(2)}, u32[]{:S(2)}) async-start(bf16[32,16,1024]{2,1,0:T(8,128)(2,1)} %get-tuple-element.10), calls=%async_computation.2 | async-start | bytes 2097152 | tf_op jit(solution)/shard_map/all_to_all | solution.py:189
  162.7 9.6 %all-to-all-start.1 = ((bf16[8,8,8,256]{3,2,1,0:T(8,128)(2,1)}), bf16[8,8,8,256]{3,2,1,0:T(8,128)(2,1)S(1)}, u32[]{:S(2)}, u32[]{:S(2)}) async-start(bf16[8,8,8,256]{3,2,1,0:T(8,128)(2,1)} %copy_bitcast_fusion), calls=%async_computation.1 | async-start | bytes 524288 | tf_op jit(solution)/shard_map/all_to_all | solution.py:187
  172.2 24.7 %all-to-all-start.3 = ((f32[256,1,128]{2,1,0:T(1,128)}), f32[256,1,128]{2,1,0:T(1,128)S(1)}, u32[]{:S(2)}, u32[]{:S(2)}) async-start(f32[256,1,128]{2,1,0:T(1,128)} %get-tuple-element.11), calls=%async_computation.3 | async-start | bytes 262144 | tf_op jit(solution)/shard_map/all_to_all | solution.py:207
  181.6 15.4 %collective-permute-start.2 = (f32[16,896]{1,0:T(8,128)S(1)}, f32[16,896]{1,0:T(8,128)S(1)}, u32[]{:S(2)}, u32[]{:S(2)}) collective-permute-start(f32[16,896]{1,0:T(8,128)S(1)} %get-tuple-element.12), channel_id=1, source_target_pairs={{0,0},{1,16},{2,32},{3,48},{4,64},{5,80},{6,96},{7,112},{8,1},{9,1... | collective-permute-start | bytes 172040 | tf_op jit(solution)/shard_map/ppermute | solution.py:206
  197.0 0.6 copy-start.7
  197.6 0.7 copy-start.6
Sparse Core Ops, SparseCore 0:
  68.5 30.7 all-gather.2

commit v2 on v1

v2 whole, which is shorter than its diff:
```python
import functools

import jax
import jax.numpy as jnp
from jax import lax
from jax.experimental import pallas as pl
from jax.experimental.pallas import tpu as pltpu
from jax.sharding import PartitionSpec as P

HEADS = 16
HEAD = 128
epsilon = 1e-06
clip_rms = 1.0
f32 = jnp.float32
bf16 = jnp.bfloat16
VMEM = pl.BlockSpec(memory_space=pltpu.VMEM)
SMEM = pl.BlockSpec(memory_space=pltpu.SMEM)
ANY = pl.BlockSpec(memory_space=pl.ANY)
MIB = 1024 * 1024


def dot(a, b, ca, cb):
    return lax.dot_general(a, b, (((ca,), (cb,)), ((), ())), preferred_element_type=f32)


def project(x, weights, gain):
    inv = lax.rsqrt(jnp.mean(x * x, axis=1, keepdims=True) + epsilon)
    normed = ((x * inv) * gain).astype(bf16)
    return normed, dot(normed, weights, 1, 1).astype(bf16)


def project_kernel(a_ref, b_ref, w_ref, gain_ref, normed_ref, proj_ref):
    gain = gain_ref[...].astype(f32)
    weights = w_ref[...]
    stretches = normed_ref.shape[0]
    per = a_ref.shape[0] // stretches
    for i, ref in enumerate((a_ref, b_ref)):
        normed, proj = project(ref[...].astype(f32), weights, gain)
        for c in range(stretches):
            normed_ref[c, i * per : (i + 1) * per, :] = normed[c * per : (c + 1) * per]
            proj_ref[c, i * per : (i + 1) * per, :] = proj[c * per : (c + 1) * per]


def project_call(first, second, weights, gain, stretches):
    rows, width = weights.shape
    per = 2 * first.shape[0] // stretches
    return pl.pallas_call(
        project_kernel,
        in_specs=[VMEM] * 4,
        out_specs=[VMEM] * 2,
        out_shape=[
            jax.ShapeDtypeStruct((stretches, per, width), bf16),
            jax.ShapeDtypeStruct((stretches, per, rows), bf16),
        ],
        compiler_params=pltpu.CompilerParams(vmem_limit_bytes=14 * MIB),
        cost_estimate=pl.CostEstimate(flops=500_000_000, bytes_accessed=4_000_000, transcendentals=512),
        name="project",
    )(first, second, weights, gain)


def main_kernel(blocks_before, me_ref, count_ref, *refs):
    normed_in, refs = refs[:blocks_before], refs[blocks_before:]
    proj_in, refs = refs[:blocks_before], refs[blocks_before:]
    a_ref, b_ref, w_ref, gain_ref, q_hbm, do_hbm, att_ref, out_ref, *refs = refs
    q_ref, do_ref, normed_ref, proj_ref, grad_ref, sems = refs
    stretches, keys, width = normed_ref.shape
    pair = 2 * HEAD
    scale = HEAD ** (-0.5)
    start = pl.multiple_of(me_ref[1] * pair, pair)
    part = normed_in[0].shape[1]
    copies = [
        pltpu.make_async_copy(q_hbm.at[:, :, pl.ds(start, pair)], q_ref, sems.at[0]),
        pltpu.make_async_copy(do_hbm.at[:, :, pl.ds(start, pair)], do_ref, sems.at[1]),
    ]
    late = []
    for i in range(blocks_before):
        here = slice(i * part, (i + 1) * part)
        copies.append(pltpu.make_async_copy(proj_in[i], proj_ref.at[:, here, :], sems.at[2 + 2 * i]))
        late.append(pltpu.make_async_copy(normed_in[i], normed_ref.at[:, here, :], sems.at[3 + 2 * i]))
    for copy in copies + late:
        copy.start()
    gain = gain_ref[...].astype(f32)
    weights_here = w_ref[...]
    per = a_ref.shape[0] // stretches
    for i, ref in enumerate((a_ref, b_ref)):
        normed, proj = project(ref[...].astype(f32), weights_here, gain)
        at = blocks_before * part + i * per
        for c in range(stretches):
            normed_ref[c, at : at + per, :] = normed[c * per : (c + 1) * per]
            proj_ref[c, at : at + per, :] = proj[c * per : (c + 1) * per]
    for copy in copies:
        copy.wait()
    lane = lax.broadcasted_iota(jnp.int32, (1, keys), 1)
    neighbour = (lane // (per // 2)) % 2
    for c in range(stretches):
        live = (neighbour < count_ref[c]).astype(f32)
        for a in range(2):
            cols = slice(a * HEAD, (a + 1) * HEAD)
            key = proj_ref[c, :, a * HEAD : (a + 1) * HEAD]
            val = proj_ref[c, :, (2 + a) * HEAD : (3 + a) * HEAD]
            q = q_ref[c, :, cols]
            do = do_ref[c, :, cols]
            weights = jnp.exp(dot(q, key, 1, 1) * scale) * live
            inv_den = 1.0 / jnp.sum(weights, axis=1, keepdims=True)
            numerator = dot(weights.astype(bf16), val, 1, 0)
            dots = dot(do, val, 1, 1)
            delta = jnp.sum(weights * dots, axis=1, keepdims=True) * inv_den
            att_ref[c, :, cols] = (numerator * inv_den).astype(bf16)
            prob = weights * inv_den
            score_grad = prob * (dots - delta)
            here = slice(c * keys, (c + 1) * keys)
            grad_ref[a * HEAD : (a + 1) * HEAD, here] = (
                dot(q, score_grad.astype(bf16), 0, 0) * scale
            ).astype(bf16)
            grad_ref[(2 + a) * HEAD : (3 + a) * HEAD, here] = dot(do, prob.astype(bf16), 0, 0).astype(bf16)
    for copy in late:
        copy.wait()
    blocks = out_ref.shape[0]
    out_ref[:, :, width:] = jnp.zeros((blocks, 16, 128), bf16)
    gain_part = jnp.zeros((1, width), f32)
    normed_all = normed_ref[...].reshape(stretches * keys, width)
    for a in range(4):
        here = slice(a * HEAD, (a + 1) * HEAD)
        raw = dot(grad_ref[here, :], normed_all, 1, 0)
        out_ref[a * 8 : (a + 1) * 8, :, :width] = raw.reshape(8, 16, width).astype(bf16)
        gain_part = gain_part + jnp.sum(raw * w_ref[here, :].astype(f32), axis=0, keepdims=True)
    gain_part = gain_part / gain
    row = lax.broadcasted_iota(jnp.int32, (16, 128), 0)
    for t in range(width // 128):
        piece = jnp.broadcast_to(gain_part[:, t * 128 : (t + 1) * 128], (16, 128))
        high = piece.astype(bf16).astype(f32)
        tile = jnp.where(row == 0, high, jnp.where(row == 1, piece - high, 0.0)).astype(bf16)
        for quarter in range(4):
            out_ref[4 * t + quarter, :, width:] = tile


def main_call(me, count, normed, proj, first, second, weights, gain, queries, d_out):
    stretches, length, _ = queries.shape
    rows, width = weights.shape
    keys = normed[0].shape[1] * (len(normed) + 1)
    blocks = rows // 16
    pair = 2 * HEAD
    return pl.pallas_call(
        functools.partial(main_kernel, len(normed)),
        in_specs=[SMEM] * 2 + [ANY] * (2 * len(normed)) + [VMEM] * 4 + [ANY] * 2,
        out_specs=[VMEM] * 2,
        out_shape=[
            jax.ShapeDtypeStruct((stretches, length, pair), bf16),
            jax.ShapeDtypeStruct((blocks, 16, width + 128), bf16),
        ],
        scratch_shapes=[
            pltpu.VMEM((stretches, length, pair), bf16),
            pltpu.VMEM((stretches, length, pair), bf16),
            pltpu.VMEM((stretches, keys, width), bf16),
            pltpu.VMEM((stretches, keys, rows), bf16),
            pltpu.VMEM((rows, stretches * keys), bf16),
            pltpu.SemaphoreType.DMA((2 + 2 * len(normed),)),
        ],
        compiler_params=pltpu.CompilerParams(vmem_limit_bytes=24 * MIB),
        cost_estimate=pl.CostEstimate(flops=4_200_000_000, bytes_accessed=8_000_000, transcendentals=262144),
        name="attend",
    )(me, count, *normed, *proj, first, second, weights, gain, queries, d_out)


def pick_kernel(at_ref, in_ref, w_ref, gain_ref, out_ref, sems):
    count = at_ref.shape[0]
    per = in_ref.shape[1]
    copies = [
        pltpu.make_async_copy(in_ref.at[at_ref[i]], out_ref.at[pl.ds(i * per, per)], sems.at[i])
        for i in range(count)
    ]
    for copy in copies:
        copy.start()
    for copy in copies:
        copy.wait()


def pick_call(at, incoming, weights, gain):
    _, per, width = incoming.shape
    return pl.pallas_call(
        pick_kernel,
        in_specs=[SMEM, ANY, ANY, ANY],
        out_specs=VMEM,
        out_shape=jax.ShapeDtypeStruct((at.shape[0] * per, width), bf16),
        scratch_shapes=[pltpu.SemaphoreType.DMA((at.shape[0],))],
        compiler_params=pltpu.CompilerParams(vmem_limit_bytes=4 * MIB),
        name="pick",
    )(at, incoming, weights, gain)


def reduce_kernel(me_ref, in_ref, red_ref, pay_ref):
    width = red_ref.shape[1]
    blocks = in_ref.shape[0]
    total = in_ref[0].astype(f32)
    for i in range(1, blocks):
        total = total + in_ref[i].astype(f32)
    red = total[:, :width]
    red_ref[...] = red
    squares = jnp.sum(jnp.sum(red * red, axis=1, keepdims=True), axis=0, keepdims=True)
    gain = total[0:1, width:] + total[1:2, width:]
    quarter = me_ref[0] % 4
    lane = lax.broadcasted_iota(jnp.int32, (1, 128), 1)
    gain = jnp.where(lane // 32 == quarter, gain, 0.0)
    pay = jnp.where(lane == ((quarter + 1) % 4) * 32, squares, gain)
    pay_ref[...] = jnp.broadcast_to(pay[None], pay_ref.shape)


def final_kernel(pay_ref, red_ref, grad_ref, gain_ref):
    blocks = 32
    pay = pay_ref[...].reshape(blocks, 8, 128)
    rows = jnp.sum(pay, axis=1)
    row = lax.broadcasted_iota(jnp.int32, (blocks, 128), 0)
    lane = lax.broadcasted_iota(jnp.int32, (blocks, 128), 1)
    gains = jnp.where((lane // 32 == row % 4) & (row < 28), rows, 0.0)
    gains = jnp.sum(gains.reshape(8, 4, 128), axis=1)
    squares = jnp.where(lane == ((row + 1) % 4) * 32, rows, 0.0)
    total = jnp.sum(jnp.sum(squares, axis=1, keepdims=True), axis=0, keepdims=True)
    total = total + jnp.sum(jnp.sum(gains * gains, axis=1, keepdims=True), axis=0, keepdims=True)
    count = 4096 * 896 + 896
    factor = jnp.minimum(1.0, clip_rms * lax.rsqrt(total / count + epsilon))
    grad_ref[...] = red_ref[...] * factor
    gains = gains * factor
    for t in range(gain_ref.shape[0] // 128):
        gain_ref[t * 128 : (t + 1) * 128] = gains[t]


def on_device(queries, d_out, database, kv_weight, gain, nbr_owner, nbr_row, nbr_count):
    groups = lax.axis_size("dp")
    shards = lax.axis_size("fsdp")
    group = lax.axis_index("dp")
    shard = lax.axis_index("fsdp")
    me = jnp.stack([group, shard]).astype(jnp.int32)
    stretches, length, head_dim = queries.shape
    per, width = database.shape[1:]
    entries = 2 * stretches
    capacity = 2
    at_group = jnp.arange(groups * stretches) // stretches
    place = jnp.arange(groups * stretches) % stretches * 2
    order = jnp.stack([place, place + 1])
    keys = order * 16 + nbr_row.T
    wanted = (nbr_owner.T == group)[None] & (at_group[None, None] == jnp.arange(groups)[:, None, None])
    first = jnp.min(jnp.where(wanted, keys[None], 256), axis=(1, 2))
    last = jnp.max(jnp.where(wanted, keys[None], 0), axis=(1, 2))
    picked = jnp.stack([first, last], axis=1) % 16
    outgoing = jnp.take(database, picked.reshape(-1), axis=0, mode="clip")
    incoming = lax.all_to_all(
        outgoing.reshape(groups, capacity, per, width), "dp", split_axis=0, concat_axis=0, tiled=True
    )
    my_owner = lax.dynamic_slice_in_dim(nbr_owner, group * stretches, stretches, 0).reshape(entries)
    earlier = jnp.arange(entries)[None, :] < jnp.arange(entries)[:, None]
    my_rank = jnp.any((my_owner[None, :] == my_owner[:, None]) & earlier, axis=1)
    half = kv_weight.shape[0] // 2
    high = shard >= shards // 2
    first, second = kv_weight[:half], kv_weight[half:]
    low_half = shards // 2
    pairs_a = [(i, 2 * i) for i in range(low_half)] + [(i + low_half, 2 * i + 1) for i in range(low_half)]
    pairs_b = [(i, 2 * i + 1) for i in range(low_half)] + [(i + low_half, 2 * i) for i in range(low_half)]
    got_a = lax.ppermute(jnp.where(high, second, first), "fsdp", pairs_a)
    got_b = lax.ppermute(jnp.where(high, first, second), "fsdp", pairs_b)
    odd = shard % 2 == 1
    weights = jnp.concatenate([jnp.where(odd, got_b, got_a), jnp.where(odd, got_a, got_b)], axis=0)
    lanes = jnp.arange(width) // gain.shape[0]
    gain_full = jnp.where(lanes == shard, jnp.tile(gain, shards), 0)[None]
    for step in (1, 2, 4):
        gain_full = gain_full + lax.ppermute(gain_full, "fsdp", [(i, i ^ step) for i in range(shards)])
    at = (my_owner * capacity + my_rank.astype(jnp.int32)).astype(jnp.int32)
    own = pick_call(at, incoming.reshape(groups * capacity, per, width), weights, gain_full)
    ring = [(i, (i + (2 if i % 2 == 0 else -2)) % shards) for i in range(shards)]
    swap = [(i, i ^ 1) for i in range(shards)]
    move = lambda block, pairs: lax.ppermute(block, "fsdp", pairs)
    near = move(own, ring)
    other = move(own, swap)
    near_b = move(other, ring)
    far = move(near, ring)
    pieces = [(own, other), (near, move(near, swap)), (near_b, move(near_b, swap))]
    done = [project_call(x, y, weights, gain_full, stretches) for x, y in pieces]
    far, done[0], done[1] = lax.optimization_barrier((far, done[0], done[1]))
    att, blocks = main_call(
        me,
        nbr_count,
        [n for n, _ in done],
        [p for _, p in done],
        far,
        move(far, swap),
        weights,
        gain_full,
        queries,
        d_out,
    )
    rows_here = length // shards
    att = att.reshape(stretches, shards, rows_here, 2 * HEAD)
    attended = jnp.zeros((stretches, rows_here, head_dim), bf16)
    for step in range(shards):
        peer = shard ^ step
        piece = lax.dynamic_index_in_dim(att, peer, 1, keepdims=False)
        if step:
            piece = lax.ppermute(piece, "fsdp", [(i, i ^ step) for i in range(shards)])
        attended = lax.dynamic_update_slice_in_dim(attended, piece, peer * 2 * HEAD, 2)
    blocks = lax.all_to_all(blocks, "dp", split_axis=0, concat_axis=0, tiled=True)
    reduced, payload = pl.pallas_call(
        reduce_kernel,
        in_specs=[SMEM, VMEM],
        out_specs=[VMEM] * 2,
        out_shape=[
            jax.ShapeDtypeStruct((16, width), f32),
            jax.ShapeDtypeStruct((groups * shards, 1, 128), f32),
        ],
        compiler_params=pltpu.CompilerParams(vmem_limit_bytes=4 * MIB),
        name="reduce",
    )(me, blocks)
    pairs = []
    for p in range(groups):
        kv, odd_head, piece = p // 16, (p // 8) % 2, p % 8
        for s in range(shards):
            pairs.append((p * shards + s, (kv * 16 + 2 * s + odd_head) * shards + piece))
    moved = lax.ppermute(reduced, ("dp", "fsdp"), pairs)
    payload = lax.all_to_all(payload, ("dp", "fsdp"), split_axis=0, concat_axis=0, tiled=True)
    kv_grad, gain_grad = pl.pallas_call(
        final_kernel,
        out_shape=[
            jax.ShapeDtypeStruct((16, width), f32),
            jax.ShapeDtypeStruct((width,), f32),
        ],
        compiler_params=pltpu.CompilerParams(vmem_limit_bytes=4 * MIB),
        name="finish",
    )(payload, moved)
    return attended, kv_grad, gain_grad


def solution(mesh):
    in_specs = (
        P("dp", None, None),
        P("dp", None, None),
        P("dp", "fsdp", None),
        P("fsdp", None),
        P("fsdp"),
        P(),
        P(),
        P("dp"),
    )
    out_specs = (P("dp", "fsdp", None), P(("dp", "fsdp"), None), P())
    return jax.shard_map(
        on_device, mesh=mesh, in_specs=in_specs, out_specs=out_specs, check_vma=False
    )
```

time: 209 us -> 154 us (0.74)
  blocking collectives: 18.4 us -> 0 us
  between operations: 14.9 us -> 1.13 us
  local copies, waits for them, and re-layouts: 15.7 us -> 3.66 us
  Pallas kernels: 24.3 us -> 15.2 us
  waiting for transfers between devices: 93.5 us -> 84.4 us
  starting transfers between devices: 39.8 us -> 45.6 us
    ppermute x0 -> x17, waiting for transfers between devices: none -> 26.8 us  [the longest x3 13.5 us: on_device(): lax.ppermute(gain_full, 'fsdp', [(i, i ^ step) for i in range(shards)])]
    all_to_all x1, waiting for transfers between devices: 43.7 us -> 23.8 us  [on_device(): lax.all_to_all(outgoing.reshape(groups, capacity, per, width), 'dp', spli...]
    unnamed x1 -> x0, blocking collectives: 18.4 us -> none
    ppermute x0 -> x17, starting transfers between devices: none -> 13.9 us  [the longest x7 7.14 us: on_device(): piece = lax.ppermute(piece, 'fsdp', [(i, i ^ step) for i in range(shards)])]
    pallas_call x2 -> x6, Pallas kernels: 22.5 us -> 14.4 us  [the longest x1 9.06 us: main_call(): pl.pallas_call(functools.partial(main_kernel, len(normed)), in_specs=[SME...]
    unnamed x25 -> x18, local copies, waits for them, and re-layouts: 9.02 us -> 1.01 us
    all_gather x1 -> x0, waiting for transfers between devices: 7.13 us -> none  [on_device(): tokens = lax.all_gather(fetched, 'fsdp', axis=0, tiled=False)]
    all_to_all x1, waiting for transfers between devices: 28 us -> 21.3 us  [on_device(): lax.all_to_all(blocks, 'dp', split_axis=0, concat_axis=0, tiled=True)]
  transfers between devices with their start and end apart: 8 -> 23, of which waited for: 5 -> 12; matrix products, arithmetic and copies ran while one was open for 2% -> 1% of each run, Pallas kernels for 1% -> 3%
where the time goes in v2:
time: 154 us; the launch traced here: 153 us
  waiting for transfers between devices  84.4 us (55%)
  starting transfers between devices  45.6 us (30%)
  Pallas kernels  15.2 us (10%)
  local copies, waits for them, and re-layouts  3.66 us (2%)
  other arithmetic  3.1 us (2%)
    all_to_all x1, waiting for transfers between devices, on_device(): lax.all_to_all(outgoing.reshape(groups, capacity, per, width), 'dp', spli...  23.8 us
    all_to_all x1, waiting for transfers between devices, on_device(): lax.all_to_all(blocks, 'dp', split_axis=0, concat_axis=0, tiled=True)  21.3 us
    ppermute x3, waiting for transfers between devices, on_device(): lax.ppermute(gain_full, 'fsdp', [(i, i ^ step) for i in range(shards)])  13.5 us
    ppermute x7, waiting for transfers between devices, on_device(): move = lambda block, pairs: lax.ppermute(block, 'fsdp', pairs)  13.1 us
    ppermute x1, waiting for transfers between devices, on_device(): moved = lax.ppermute(reduced, ('dp', 'fsdp'), pairs)  12.5 us
    all_to_all x1, starting transfers between devices, on_device(): lax.all_to_all(outgoing.reshape(groups, capacity, per, width), 'dp', spli...  11.3 us
    pallas_call x1, Pallas kernels, main_call(): pl.pallas_call(functools.partial(main_kernel, len(normed)), in_specs=[SME...  9.06 us
    all_to_all x1, starting transfers between devices, on_device(): lax.all_to_all(payload, ('dp', 'fsdp'), split_axis=0, concat_axis=0, tile...  8.47 us
  transfers between devices with their start and end apart: 23, of which 12 were waited for; matrix products, arithmetic and copies ran while one was open for 1% of the time, Pallas kernels for 3%

profile of v2, /device:TPU:48, one launch (start us, length us, event | category | flops | bytes accessed | tf_op | source)
XLA Modules:
  0.0 153.2 jit_solution(11530544545583769296)
XLA Ops:
  2.5 2.0 %gather_fusion = bf16[64,16,896]{2,1,0:T(8,128)(2,1)} fusion(bf16[16,16,896]{2,1,0:T(8,128)(2,1)S(1)} %copy-done, s32[1024]{0:T(1024)S(1)} %pad_clamp_fusion), kind=kCustom, calls=%fused_computation | custom fusion | bytes 3670272 | tf_op jit(solution)/shard_map/jit(_take)/gather | solution.py:245
  4.5 11.3 %all-to-all-start = ((bf16[32,2,16,896]{3,2,1,0:T(8,128)(2,1)}), bf16[32,2,16,896]{3,2,1,0:T(8,128)(2,1)S(1)}, u32[]{:S(2)}, u32[]{:S(2)}) async-start(bf16[32,2,16,896]{3,2,1,0:T(8,128)(2,1)} %bitcast.32), calls=%async_computation | async-start | bytes 3670016 | tf_op jit(solution)/shard_map/all_to_all | solution.py:246
  15.9 1.0 broadcast_select_fusion.1
  17.2 2.1 %collective-permute-start.1 = (bf16[256,896]{1,0:T(8,128)(2,1)}, bf16[256,896]{1,0:T(8,128)(2,1)S(1)}, u32[]{:S(2)}, u32[]{:S(2)}) collective-permute-start(bf16[256,896]{1,0:T(8,128)(2,1)} %get-tuple-element.42), channel_id=1, source_target_pairs={{0,0},{1,2},{2,4},{3,6},{4,1},{5,3},{6,5},{7,7},{8,8},{9,10},{10,1... | collective-permute-start | bytes 1376264 | tf_op jit(solution)/shard_map/ppermute | solution.py:258
  19.4 1.0 collective-permute-start.2
  21.3 1.2 collective-permute-start.3
  22.7 7.9 %collective-permute-done.3 = bf16[1,896]{1,0:T(2,128)(2,1)S(1)} collective-permute-done((bf16[1,896]{1,0:T(2,128)(2,1)S(1)}, bf16[1,896]{1,0:T(2,128)(2,1)S(1)}, u32[]{:S(2)}, u32[]{:S(2)}) %collective-permute-start.3) | collective-permute-done | bytes 1824 | tf_op jit(solution)/shard_map/ppermute | solution.py:265
  30.7 5.1 %collective-permute-done.4 = bf16[1,896]{1,0:T(2,128)(2,1)S(1)} collective-permute-done((bf16[1,896]{1,0:T(2,128)(2,1)S(1)}, bf16[1,896]{1,0:T(2,128)(2,1)S(1)}, u32[]{:S(2)}, u32[]{:S(2)}) %collective-permute-start.4) | collective-permute-done | bytes 1824 | tf_op jit(solution)/shard_map/ppermute | solution.py:265
  36.0 23.8 %all-to-all-done = bf16[32,2,16,896]{3,2,1,0:T(8,128)(2,1)S(1)} async-done(((bf16[32,2,16,896]{3,2,1,0:T(8,128)(2,1)}), bf16[32,2,16,896]{3,2,1,0:T(8,128)(2,1)S(1)}, u32[]{:S(2)}, u32[]{:S(2)}) %all-to-all-start) | async-done | bytes 1835040 | tf_op jit(solution)/shard_map/all_to_all | solution.py:246
  59.7 1.3 pick.1.a_ref
  61.2 1.4 collective-permute-start.5
  63.0 1.3 collective-permute-start.9
  64.3 5.5 %collective-permute-done.5.a_ref = bf16[256,896]{1,0:T(8,128)(2,1)S(1)} collective-permute-done((bf16[256,896]{1,0:T(8,128)(2,1)S(1)}, bf16[256,896]{1,0:T(8,128)(2,1)S(1)}, u32[]{:S(2)}, u32[]{:S(2)}) %collective-permute-start.5) | collective-permute-done | bytes 458784 | tf_op jit(solution)/shard_map/ppermute | solution.py:270
  69.7 1.8 %collective-permute-start.6 = (bf16[256,896]{1,0:T(8,128)(2,1)S(1)}, bf16[256,896]{1,0:T(8,128)(2,1)S(1)}, u32[]{:S(2)}, u32[]{:S(2)}) collective-permute-start(bf16[256,896]{1,0:T(8,128)(2,1)S(1)} %collective-permute-done.5.a_ref), channel_id=1, source_target_pairs={{0,2},{1,7},{2,4},{3,1},{4,6},{5,3},{6,0},{7,5},{8,10},{9,15},{10,... | collective-permute-start | bytes 1376264 | tf_op jit(solution)/shard_map/ppermute | solution.py:270
  71.5 0.8 project.3
  72.4 2.3 %collective-permute-done.9.a_ref = bf16[256,896]{1,0:T(8,128)(2,1)S(1)} collective-permute-done((bf16[256,896]{1,0:T(8,128)(2,1)S(1)}, bf16[256,896]{1,0:T(8,128)(2,1)S(1)}, u32[]{:S(2)}, u32[]{:S(2)}) %collective-permute-start.9) | collective-permute-done | bytes 458784 | tf_op jit(solution)/shard_map/ppermute | solution.py:270
  74.7 0.9 project.4
  75.5 4.0 %collective-permute-done.6.refs_6_ = bf16[256,896]{1,0:T(8,128)(2,1)S(1)} collective-permute-done((bf16[256,896]{1,0:T(8,128)(2,1)S(1)}, bf16[256,896]{1,0:T(8,128)(2,1)S(1)}, u32[]{:S(2)}, u32[]{:S(2)}) %collective-permute-start.6) | collective-permute-done | bytes 458784 | tf_op jit(solution)/shard_map/ppermute | solution.py:270
  79.7 0.9 project.5
  80.5 0.9 collective-permute-done.11.refs_7_
  81.4 9.1 %attend.1 = (bf16[8,64,256]{2,1,0:T(8,128)(2,1)S(1)}, bf16[32,16,1024]{2,1,0:T(8,128)(2,1)S(1)}) custom-call(s32[2]{0:T(128)S(1)} %pad_add_fusion.1.me_ref, s32[8]{0:T(128)S(1)} %copy-done.4, bf16[8,64,896]{2,1,0:T(8,128)(2,1)S(1)} %get-tuple-element.24.refs_0_, bf16[8,64,896]{2,1,0:T(8,128)(2,1)S(1)} %get-tuple-element.25.refs_1_, ...), custom_call_target="tpu_custom_call" | custom-call | flops 4200000000 | bytes 8000000 | tf_op jit(solution)/shard_map/attend/pallas_call | solution.py:143
  90.5 1.0 copy-done.1
  91.4 6.6 %all-to-all-start.1 = ((bf16[32,16,1024]{2,1,0:T(8,128)(2,1)}), bf16[32,16,1024]{2,1,0:T(8,128)(2,1)S(1)}, u32[]{:S(2)}, u32[]{:S(2)}) async-start(bf16[32,16,1024]{2,1,0:T(8,128)(2,1)} %copy-done.1), calls=%async_computation.1 | async-start | bytes 2097152 | tf_op jit(solution)/shard_map/all_to_all | solution.py:299
  98.3 1.5 collective-permute-start.13
  100.2 1.6 %collective-permute-start.15 = (bf16[8,8,256]{2,1,0:T(8,128)(2,1)S(1)}, bf16[8,8,256]{2,1,0:T(8,128)(2,1)S(1)}, u32[]{:S(2)}, u32[]{:S(2)}) collective-permute-start(bf16[8,8,256]{2,1,0:T(8,128)(2,1)S(1)} %get-tuple-element.46), channel_id=1, source_target_pairs={{0,4},{1,5},{2,6},{3,7},{4,0},{5,1},{6,2},{7,3},{8,12},{9,13},{10,... | collective-permute-start | bytes 98312 | tf_op jit(solution)/shard_map/ppermute | solution.py:297
  101.7 1.7 %collective-permute-start.16 = (bf16[8,8,256]{2,1,0:T(8,128)(2,1)S(1)}, bf16[8,8,256]{2,1,0:T(8,128)(2,1)S(1)}, u32[]{:S(2)}, u32[]{:S(2)}) collective-permute-start(bf16[8,8,256]{2,1,0:T(8,128)(2,1)S(1)} %get-tuple-element.45), channel_id=1, source_target_pairs={{0,5},{1,4},{2,7},{3,6},{4,1},{5,0},{6,3},{7,2},{8,13},{9,12},{10,... | collective-permute-start | bytes 98312 | tf_op jit(solution)/shard_map/ppermute | solution.py:297
  104.0 1.4 collective-permute-start.18
  105.6 21.3 %all-to-all-done.1.in_ref = bf16[32,16,1024]{2,1,0:T(8,128)(2,1)S(1)} async-done(((bf16[32,16,1024]{2,1,0:T(8,128)(2,1)}), bf16[32,16,1024]{2,1,0:T(8,128)(2,1)S(1)}, u32[]{:S(2)}, u32[]{:S(2)}) %all-to-all-start.1) | async-done | bytes 1048608 | tf_op jit(solution)/shard_map/all_to_all | solution.py:299
  126.9 1.5 reduce.1
  128.4 8.5 %all-to-all-start.2 = ((f32[256,1,128]{2,1,0:T(1,128)}), f32[256,1,128]{2,1,0:T(1,128)S(1)}, u32[]{:S(2)}, u32[]{:S(2)}) async-start(f32[256,1,128]{2,1,0:T(1,128)} %get-tuple-element.33), calls=%async_computation.2 | async-start | bytes 262144 | tf_op jit(solution)/shard_map/all_to_all | solution.py:317
  136.9 2.9 %collective-permute-start.19 = (f32[16,896]{1,0:T(8,128)S(1)}, f32[16,896]{1,0:T(8,128)S(1)}, u32[]{:S(2)}, u32[]{:S(2)}) collective-permute-start(f32[16,896]{1,0:T(8,128)S(1)} %get-tuple-element.34), channel_id=1, source_target_pairs={{0,0},{1,16},{2,32},{3,48},{4,64},{5,80},{6,96},{7,112},{8,1},{9,1... | collective-permute-start | bytes 172040 | tf_op jit(solution)/shard_map/ppermute | solution.py:316
  139.8 12.5 %collective-permute-done.19.red_ref = f32[16,896]{1,0:T(8,128)S(1)} collective-permute-done((f32[16,896]{1,0:T(8,128)S(1)}, f32[16,896]{1,0:T(8,128)S(1)}, u32[]{:S(2)}, u32[]{:S(2)}) %collective-permute-start.19) | collective-permute-done | bytes 57376 | tf_op jit(solution)/shard_map/ppermute | solution.py:316
  (76 shorter events, 6.4 us)
Async XLA Ops:
  0.6 1.9 %copy-start = (bf16[16,16,896]{2,1,0:T(8,128)(2,1)S(1)}, bf16[16,16,896]{2,1,0:T(8,128)(2,1)}, u32[]{:S(2)}) copy-start(bf16[16,16,896]{2,1,0:T(8,128)(2,1)} %param.10) | copy-start | bytes 1376260
  4.5 11.4 %copy-start.5 = (bf16[512,896]{1,0:T(8,128)(2,1)S(1)}, bf16[512,896]{1,0:T(8,128)(2,1)}, u32[]{:S(2)}) copy-start(bf16[512,896]{1,0:T(8,128)(2,1)} %param.11) | copy-start | bytes 2752516
  4.5 55.3 %all-to-all-start = ((bf16[32,2,16,896]{3,2,1,0:T(8,128)(2,1)}), bf16[32,2,16,896]{3,2,1,0:T(8,128)(2,1)S(1)}, u32[]{:S(2)}, u32[]{:S(2)}) async-start(bf16[32,2,16,896]{3,2,1,0:T(8,128)(2,1)} %bitcast.32), calls=%async_computation | async-start | bytes 3670016 | tf_op jit(solution)/shard_map/all_to_all | solution.py:246
  15.8 3.5 %copy-start.8 = (bf16[112]{0:T(256)(128)(2,1)S(1)}, bf16[112]{0:T(256)(128)(2,1)}, u32[]{:S(2)}) copy-start(bf16[112]{0:T(256)(128)(2,1)} %param.12) | copy-start | bytes 676
  15.8 4.6 %copy-start.7 = (s32[256,2]{0,1:T(2,128)S(1)}, s32[256,2]{0,1:T(2,128)}, u32[]{:S(2)}) copy-start(s32[256,2]{0,1:T(2,128)} %param.13) | copy-start | bytes 6148
  16.9 18.9 %collective-permute-start = (bf16[256,896]{1,0:T(8,128)(2,1)}, bf16[256,896]{1,0:T(8,128)(2,1)S(1)}, u32[]{:S(2)}, u32[]{:S(2)}) collective-permute-start(bf16[256,896]{1,0:T(8,128)(2,1)} %get-tuple-element.41), channel_id=1, source_target_pairs={{0,1},{1,3},{2,5},{3,7},{4,0},{5,2},{6,4},{7,6},{8,9},{9,11},{10,1... | collective-permute-start | bytes 1376264 | tf_op jit(solution)/shard_map/ppermute | solution.py:259
  17.2 18.6 %collective-permute-start.1 = (bf16[256,896]{1,0:T(8,128)(2,1)}, bf16[256,896]{1,0:T(8,128)(2,1)S(1)}, u32[]{:S(2)}, u32[]{:S(2)}) collective-permute-start(bf16[256,896]{1,0:T(8,128)(2,1)} %get-tuple-element.42), channel_id=1, source_target_pairs={{0,0},{1,2},{2,4},{3,6},{4,1},{5,3},{6,5},{7,7},{8,8},{9,10},{10,1... | collective-permute-start | bytes 1376264 | tf_op jit(solution)/shard_map/ppermute | solution.py:258
  19.4 1.9 %collective-permute-start.2 = (bf16[1,896]{1,0:T(2,128)(2,1)S(1)}, bf16[1,896]{1,0:T(2,128)(2,1)S(1)}, u32[]{:S(2)}, u32[]{:S(2)}) collective-permute-start(bf16[1,896]{1,0:T(2,128)(2,1)S(1)} %compare_select_fusion), channel_id=1, source_target_pairs={{0,1},{1,0},{2,3},{3,2},{4,5},{5,4},{6,7},{7,6},{8,9},{9,8},{10,11... | collective-permute-start | bytes 5384 | tf_op jit(solution)/shard_map/ppermute | solution.py:265
  21.3 9.2 %collective-permute-start.3 = (bf16[1,896]{1,0:T(2,128)(2,1)S(1)}, bf16[1,896]{1,0:T(2,128)(2,1)S(1)}, u32[]{:S(2)}, u32[]{:S(2)}) collective-permute-start(bf16[1,896]{1,0:T(2,128)(2,1)S(1)} %fusion.8), channel_id=1, source_target_pairs={{0,2},{1,3},{2,0},{3,1},{4,6},{5,7},{6,4},{7,5},{8,10},{9,11},{10,... | collective-permute-start | bytes 5384 | tf_op jit(solution)/shard_map/ppermute | solution.py:265
  30.6 5.2 %collective-permute-start.4 = (bf16[1,896]{1,0:T(2,128)(2,1)S(1)}, bf16[1,896]{1,0:T(2,128)(2,1)S(1)}, u32[]{:S(2)}, u32[]{:S(2)}) collective-permute-start(bf16[1,896]{1,0:T(2,128)(2,1)S(1)} %add.135), channel_id=1, source_target_pairs={{0,4},{1,5},{2,6},{3,7},{4,0},{5,1},{6,2},{7,3},{8,12},{9,13},{10,... | collective-permute-start | bytes 5384 | tf_op jit(solution)/shard_map/ppermute | solution.py:265
  61.1 1.9 %collective-permute-start.7 = (bf16[256,896]{1,0:T(8,128)(2,1)S(1)}, bf16[256,896]{1,0:T(8,128)(2,1)S(1)}, u32[]{:S(2)}, u32[]{:S(2)}) collective-permute-start(bf16[256,896]{1,0:T(8,128)(2,1)S(1)} %pick.1.a_ref), channel_id=1, source_target_pairs={{0,1},{1,0},{2,3},{3,2},{4,5},{5,4},{6,7},{7,6},{8,9},{9,8},{10,11... | collective-permute-start | bytes 1376264 | tf_op jit(solution)/shard_map/ppermute | solution.py:270
  61.2 8.6 %collective-permute-start.5 = (bf16[256,896]{1,0:T(8,128)(2,1)S(1)}, bf16[256,896]{1,0:T(8,128)(2,1)S(1)}, u32[]{:S(2)}, u32[]{:S(2)}) collective-permute-start(bf16[256,896]{1,0:T(8,128)(2,1)S(1)} %pick.1.a_ref), channel_id=1, source_target_pairs={{0,2},{1,7},{2,4},{3,1},{4,6},{5,3},{6,0},{7,5},{8,10},{9,15},{10,... | collective-permute-start | bytes 1376264 | tf_op jit(solution)/shard_map/ppermute | solution.py:270
  63.0 11.7 %collective-permute-start.9 = (bf16[256,896]{1,0:T(8,128)(2,1)S(1)}, bf16[256,896]{1,0:T(8,128)(2,1)S(1)}, u32[]{:S(2)}, u32[]{:S(2)}) collective-permute-start(bf16[256,896]{1,0:T(8,128)(2,1)S(1)} %collective-permute-done.7.b_ref), channel_id=1, source_target_pairs={{0,2},{1,7},{2,4},{3,1},{4,6},{5,3},{6,0},{7,5},{8,10},{9,15},{10,... | collective-permute-start | bytes 1376264 | tf_op jit(solution)/shard_map/ppermute | solution.py:270
  69.7 4.9 %collective-permute-start.8 = (bf16[256,896]{1,0:T(8,128)(2,1)S(1)}, bf16[256,896]{1,0:T(8,128)(2,1)S(1)}, u32[]{:S(2)}, u32[]{:S(2)}) collective-permute-start(bf16[256,896]{1,0:T(8,128)(2,1)S(1)} %collective-permute-done.5.a_ref), channel_id=1, source_target_pairs={{0,1},{1,0},{2,3},{3,2},{4,5},{5,4},{6,7},{7,6},{8,9},{9,8},{10,11... | collective-permute-start | bytes 1376264 | tf_op jit(solution)/shard_map/ppermute | solution.py:270
  69.7 9.8 %collective-permute-start.6 = (bf16[256,896]{1,0:T(8,128)(2,1)S(1)}, bf16[256,896]{1,0:T(8,128)(2,1)S(1)}, u32[]{:S(2)}, u32[]{:S(2)}) collective-permute-start(bf16[256,896]{1,0:T(8,128)(2,1)S(1)} %collective-permute-done.5.a_ref), channel_id=1, source_target_pairs={{0,2},{1,7},{2,4},{3,1},{4,6},{5,3},{6,0},{7,5},{8,10},{9,15},{10,... | collective-permute-start | bytes 1376264 | tf_op jit(solution)/shard_map/ppermute | solution.py:270
  71.5 9.9 %copy-start.3 = (bf16[8,64,2048]{2,1,0:T(8,128)(2,1)S(1)}, bf16[8,64,2048]{2,1,0:T(8,128)(2,1)}, u32[]{:S(2)}) copy-start(bf16[8,64,2048]{2,1,0:T(8,128)(2,1)} %refs_11_.1) | copy-start | bytes 6291460
  72.4 9.0 %copy-start.2 = (bf16[8,64,2048]{2,1,0:T(8,128)(2,1)S(1)}, bf16[8,64,2048]{2,1,0:T(8,128)(2,1)}, u32[]{:S(2)}) copy-start(bf16[8,64,2048]{2,1,0:T(8,128)(2,1)} %refs_10_.1) | copy-start | bytes 6291460
  72.4 9.0 %copy-start.4 = (s32[8]{0:T(128)S(1)}, s32[8]{0:T(128)}, u32[]{:S(2)}) copy-start(s32[8]{0:T(128)} %count_ref.1) | copy-start | bytes 100
  74.7 5.0 %collective-permute-start.10 = (bf16[256,896]{1,0:T(8,128)(2,1)S(1)}, bf16[256,896]{1,0:T(8,128)(2,1)S(1)}, u32[]{:S(2)}, u32[]{:S(2)}) collective-permute-start(bf16[256,896]{1,0:T(8,128)(2,1)S(1)} %collective-permute-done.9.a_ref), channel_id=1, source_target_pairs={{0,1},{1,0},{2,3},{3,2},{4,5},{5,4},{6,7},{7,6},{8,9},{9,8},{10,11... | collective-permute-start | bytes 1376264 | tf_op jit(solution)/shard_map/ppermute | solution.py:270
  79.6 1.8 %collective-permute-start.11 = (bf16[256,896]{1,0:T(8,128)(2,1)S(1)}, bf16[256,896]{1,0:T(8,128)(2,1)S(1)}, u32[]{:S(2)}, u32[]{:S(2)}) collective-permute-start(bf16[256,896]{1,0:T(8,128)(2,1)S(1)} %collective-permute-done.6.refs_6_), channel_id=1, source_target_pairs={{0,1},{1,0},{2,3},{3,2},{4,5},{5,4},{6,7},{7,6},{8,9},{9,8},{10,11... | collective-permute-start | bytes 1376264 | tf_op jit(solution)/shard_map/ppermute | solution.py:270
  90.5 1.0 copy-start.1
  91.4 35.5 %all-to-all-start.1 = ((bf16[32,16,1024]{2,1,0:T(8,128)(2,1)}), bf16[32,16,1024]{2,1,0:T(8,128)(2,1)S(1)}, u32[]{:S(2)}, u32[]{:S(2)}) async-start(bf16[32,16,1024]{2,1,0:T(8,128)(2,1)} %copy-done.1), calls=%async_computation.1 | async-start | bytes 2097152 | tf_op jit(solution)/shard_map/all_to_all | solution.py:299
  98.2 5.2 %collective-permute-start.12 = (bf16[8,8,256]{2,1,0:T(8,128)(2,1)S(1)}, bf16[8,8,256]{2,1,0:T(8,128)(2,1)S(1)}, u32[]{:S(2)}, u32[]{:S(2)}) collective-permute-start(bf16[8,8,256]{2,1,0:T(8,128)(2,1)S(1)} %get-tuple-element.49), channel_id=1, source_target_pairs={{0,1},{1,0},{2,3},{3,2},{4,5},{5,4},{6,7},{7,6},{8,9},{9,8},{10,11... | collective-permute-start | bytes 98312 | tf_op jit(solution)/shard_map/ppermute | solution.py:297
  98.3 5.7 %collective-permute-start.13 = (bf16[8,8,256]{2,1,0:T(8,128)(2,1)S(1)}, bf16[8,8,256]{2,1,0:T(8,128)(2,1)S(1)}, u32[]{:S(2)}, u32[]{:S(2)}) collective-permute-start(bf16[8,8,256]{2,1,0:T(8,128)(2,1)S(1)} %get-tuple-element.48), channel_id=1, source_target_pairs={{0,2},{1,3},{2,0},{3,1},{4,6},{5,7},{6,4},{7,5},{8,10},{9,11},{10,... | collective-permute-start | bytes 98312 | tf_op jit(solution)/shard_map/ppermute | solution.py:297
  99.8 5.6 %collective-permute-start.14 = (bf16[8,8,256]{2,1,0:T(8,128)(2,1)S(1)}, bf16[8,8,256]{2,1,0:T(8,128)(2,1)S(1)}, u32[]{:S(2)}, u32[]{:S(2)}) collective-permute-start(bf16[8,8,256]{2,1,0:T(8,128)(2,1)S(1)} %get-tuple-element.47), channel_id=1, source_target_pairs={{0,3},{1,2},{2,1},{3,0},{4,7},{5,6},{6,5},{7,4},{8,11},{9,10},{10,... | collective-permute-start | bytes 98312 | tf_op jit(solution)/shard_map/ppermute | solution.py:297
  100.2 5.4 %collective-permute-start.15 = (bf16[8,8,256]{2,1,0:T(8,128)(2,1)S(1)}, bf16[8,8,256]{2,1,0:T(8,128)(2,1)S(1)}, u32[]{:S(2)}, u32[]{:S(2)}) collective-permute-start(bf16[8,8,256]{2,1,0:T(8,128)(2,1)S(1)} %get-tuple-element.46), channel_id=1, source_target_pairs={{0,4},{1,5},{2,6},{3,7},{4,0},{5,1},{6,2},{7,3},{8,12},{9,13},{10,... | collective-permute-start | bytes 98312 | tf_op jit(solution)/shard_map/ppermute | solution.py:297
  101.7 35.1 %collective-permute-start.16 = (bf16[8,8,256]{2,1,0:T(8,128)(2,1)S(1)}, bf16[8,8,256]{2,1,0:T(8,128)(2,1)S(1)}, u32[]{:S(2)}, u32[]{:S(2)}) collective-permute-start(bf16[8,8,256]{2,1,0:T(8,128)(2,1)S(1)} %get-tuple-element.45), channel_id=1, source_target_pairs={{0,5},{1,4},{2,7},{3,6},{4,1},{5,0},{6,3},{7,2},{8,13},{9,12},{10,... | collective-permute-start | bytes 98312 | tf_op jit(solution)/shard_map/ppermute | solution.py:297
  103.5 33.4 %collective-permute-start.17 = (bf16[8,8,256]{2,1,0:T(8,128)(2,1)S(1)}, bf16[8,8,256]{2,1,0:T(8,128)(2,1)S(1)}, u32[]{:S(2)}, u32[]{:S(2)}) collective-permute-start(bf16[8,8,256]{2,1,0:T(8,128)(2,1)S(1)} %get-tuple-element.44), channel_id=1, source_target_pairs={{0,6},{1,7},{2,4},{3,5},{4,2},{5,3},{6,0},{7,1},{8,14},{9,15},{10,... | collective-permute-start | bytes 98312 | tf_op jit(solution)/shard_map/ppermute | solution.py:297
  104.0 35.8 %collective-permute-start.18 = (bf16[8,8,256]{2,1,0:T(8,128)(2,1)S(1)}, bf16[8,8,256]{2,1,0:T(8,128)(2,1)S(1)}, u32[]{:S(2)}, u32[]{:S(2)}) collective-permute-start(bf16[8,8,256]{2,1,0:T(8,128)(2,1)S(1)} %get-tuple-element.43), channel_id=1, source_target_pairs={{0,7},{1,6},{2,5},{3,4},{4,3},{5,2},{6,1},{7,0},{8,15},{9,14},{10,... | collective-permute-start | bytes 98312 | tf_op jit(solution)/shard_map/ppermute | solution.py:297
  128.4 24.0 %all-to-all-start.2 = ((f32[256,1,128]{2,1,0:T(1,128)}), f32[256,1,128]{2,1,0:T(1,128)S(1)}, u32[]{:S(2)}, u32[]{:S(2)}) async-start(f32[256,1,128]{2,1,0:T(1,128)} %get-tuple-element.33), calls=%async_computation.2 | async-start | bytes 262144 | tf_op jit(solution)/shard_map/all_to_all | solution.py:317
  136.9 15.4 %collective-permute-start.19 = (f32[16,896]{1,0:T(8,128)S(1)}, f32[16,896]{1,0:T(8,128)S(1)}, u32[]{:S(2)}, u32[]{:S(2)}) collective-permute-start(f32[16,896]{1,0:T(8,128)S(1)} %get-tuple-element.34), channel_id=1, source_target_pairs={{0,0},{1,16},{2,32},{3,48},{4,64},{5,80},{6,96},{7,112},{8,1},{9,1... | collective-permute-start | bytes 172040 | tf_op jit(solution)/shard_map/ppermute | solution.py:316
  139.8 13.4 %copy-start.6 = (bf16[8,8,2048]{2,1,0:T(8,128)(2,1)}, bf16[8,8,2048]{2,1,0:T(8,128)(2,1)S(1)}, u32[]{:S(2)}) copy-start(bf16[8,8,2048]{2,1,0:T(8,128)(2,1)S(1)} %constant_dynamic-update-slice_fusion) | copy-start | bytes 786436

commit v3 on v2

--- a/solution.py
+++ b/solution.py
@@ -61,23 +61,22 @@
 def main_kernel(blocks_before, me_ref, count_ref, *refs):
     normed_in, refs = refs[:blocks_before], refs[blocks_before:]
     proj_in, refs = refs[:blocks_before], refs[blocks_before:]
-    a_ref, b_ref, w_ref, gain_ref, q_hbm, do_hbm, att_ref, out_ref, *refs = refs
-    q_ref, do_ref, normed_ref, proj_ref, grad_ref, sems = refs
+    a_ref, b_ref, w_ref, gain_ref, q_hbm, do_hbm, att_ref, out_ref, part_ref, *refs = refs
+    q_ref, do_ref, normed_ref, proj_ref, grad_ref, stage_ref, in_sems, out_sems = refs
     stretches, keys, width = normed_ref.shape
+    scale = HEAD ** (-0.5)
+    part = normed_in[0].shape[1]
     pair = 2 * HEAD
-    scale = HEAD ** (-0.5)
     start = pl.multiple_of(me_ref[1] * pair, pair)
-    part = normed_in[0].shape[1]
+    early = [
+        pltpu.make_async_copy(q_hbm.at[:, :, pl.ds(start, pair)], q_ref, in_sems.at[blocks_before]),
+        pltpu.make_async_copy(do_hbm.at[:, :, pl.ds(start, pair)], do_ref, in_sems.at[blocks_before + 1]),
+    ]
     copies = [
-        pltpu.make_async_copy(q_hbm.at[:, :, pl.ds(start, pair)], q_ref, sems.at[0]),
-        pltpu.make_async_copy(do_hbm.at[:, :, pl.ds(start, pair)], do_ref, sems.at[1]),
+        pltpu.make_async_copy(ref, normed_ref.at[:, i * part : (i + 1) * part, :], in_sems.at[i])
+        for i, ref in enumerate(normed_in)
     ]
-    late = []
-    for i in range(blocks_before):
-        here = slice(i * part, (i + 1) * part)
-        copies.append(pltpu.make_async_copy(proj_in[i], proj_ref.at[:, here, :], sems.at[2 + 2 * i]))
-        late.append(pltpu.make_async_copy(normed_in[i], normed_ref.at[:, here, :], sems.at[3 + 2 * i]))
-    for copy in copies + late:
+    for copy in early + copies:
         copy.start()
     gain = gain_ref[...].astype(f32)
     weights_here = w_ref[...]
@@ -87,17 +86,19 @@
         at = blocks_before * part + i * per
         for c in range(stretches):
             normed_ref[c, at : at + per, :] = normed[c * per : (c + 1) * per]
-            proj_ref[c, at : at + per, :] = proj[c * per : (c + 1) * per]
-    for copy in copies:
+            proj_ref[c, i * per : (i + 1) * per, :] = proj[c * per : (c + 1) * per]
+    for copy in early:
         copy.wait()
+    proj_all = (*proj_in, proj_ref)
     lane = lax.broadcasted_iota(jnp.int32, (1, keys), 1)
     neighbour = (lane // (per // 2)) % 2
     for c in range(stretches):
         live = (neighbour < count_ref[c]).astype(f32)
         for a in range(2):
             cols = slice(a * HEAD, (a + 1) * HEAD)
-            key = proj_ref[c, :, a * HEAD : (a + 1) * HEAD]
-            val = proj_ref[c, :, (2 + a) * HEAD : (3 + a) * HEAD]
+            val_cols = slice((2 + a) * HEAD, (3 + a) * HEAD)
+            key = jnp.concatenate([ref[c, :, cols] for ref in proj_all], axis=0)
+            val = jnp.concatenate([ref[c, :, val_cols] for ref in proj_all], axis=0)
             q = q_ref[c, :, cols]
             do = do_ref[c, :, cols]
             weights = jnp.exp(dot(q, key, 1, 1) * scale) * live
@@ -109,54 +110,55 @@
             prob = weights * inv_den
             score_grad = prob * (dots - delta)
             here = slice(c * keys, (c + 1) * keys)
-            grad_ref[a * HEAD : (a + 1) * HEAD, here] = (
-                dot(q, score_grad.astype(bf16), 0, 0) * scale
-            ).astype(bf16)
-            grad_ref[(2 + a) * HEAD : (3 + a) * HEAD, here] = dot(do, prob.astype(bf16), 0, 0).astype(bf16)
-    for copy in late:
+            grad_ref[cols, here] = (dot(q, score_grad.astype(bf16), 0, 0) * scale).astype(bf16)
+            grad_ref[val_cols, here] = dot(do, prob.astype(bf16), 0, 0).astype(bf16)
+    for copy in copies:
         copy.wait()
-    blocks = out_ref.shape[0]
-    out_ref[:, :, width:] = jnp.zeros((blocks, 16, 128), bf16)
     gain_part = jnp.zeros((1, width), f32)
     normed_all = normed_ref[...].reshape(stretches * keys, width)
+    sends = []
     for a in range(4):
         here = slice(a * HEAD, (a + 1) * HEAD)
         raw = dot(grad_ref[here, :], normed_all, 1, 0)
-        out_ref[a * 8 : (a + 1) * 8, :, :width] = raw.reshape(8, 16, width).astype(bf16)
+        stage_ref[a] = raw.reshape(8, 16, width).astype(bf16)
+        sends.append(
+            pltpu.make_async_copy(stage_ref.at[a], out_ref.at[pl.ds(a * 8, 8)], out_sems.at[a])
+        )
+        sends[a].start()
         gain_part = gain_part + jnp.sum(raw * w_ref[here, :].astype(f32), axis=0, keepdims=True)
-    gain_part = gain_part / gain
-    row = lax.broadcasted_iota(jnp.int32, (16, 128), 0)
-    for t in range(width // 128):
-        piece = jnp.broadcast_to(gain_part[:, t * 128 : (t + 1) * 128], (16, 128))
-        high = piece.astype(bf16).astype(f32)
-        tile = jnp.where(row == 0, high, jnp.where(row == 1, piece - high, 0.0)).astype(bf16)
-        for quarter in range(4):
-            out_ref[4 * t + quarter, :, width:] = tile
+    part_ref[...] = gain_part / gain
+    for send in sends:
+        send.wait()
 
 
 def main_call(me, count, normed, proj, first, second, weights, gain, queries, d_out):
     stretches, length, _ = queries.shape
+    pair = 2 * HEAD
     rows, width = weights.shape
-    keys = normed[0].shape[1] * (len(normed) + 1)
+    before = len(normed)
+    part = normed[0].shape[1]
+    keys = part * (before + 1)
     blocks = rows // 16
-    pair = 2 * HEAD
     return pl.pallas_call(
-        functools.partial(main_kernel, len(normed)),
-        in_specs=[SMEM] * 2 + [ANY] * (2 * len(normed)) + [VMEM] * 4 + [ANY] * 2,
-        out_specs=[VMEM] * 2,
+        functools.partial(main_kernel, before),
+        in_specs=[SMEM] * 2 + [ANY] * before + [VMEM] * (before + 4) + [ANY] * 2,
+        out_specs=[VMEM, pl.BlockSpec(memory_space=pltpu.HBM), VMEM],
         out_shape=[
             jax.ShapeDtypeStruct((stretches, length, pair), bf16),
-            jax.ShapeDtypeStruct((blocks, 16, width + 128), bf16),
+            jax.ShapeDtypeStruct((blocks, 16, width), bf16),
+            jax.ShapeDtypeStruct((1, width), f32),
         ],
         scratch_shapes=[
             pltpu.VMEM((stretches, length, pair), bf16),
             pltpu.VMEM((stretches, length, pair), bf16),
             pltpu.VMEM((stretches, keys, width), bf16),
-            pltpu.VMEM((stretches, keys, rows), bf16),
+            pltpu.VMEM((stretches, part, rows), bf16),
             pltpu.VMEM((rows, stretches * keys), bf16),
-            pltpu.SemaphoreType.DMA((2 + 2 * len(normed),)),
-        ],
-        compiler_params=pltpu.CompilerParams(vmem_limit_bytes=24 * MIB),
+            pltpu.VMEM((4, 8, 16, width), bf16),
+            pltpu.SemaphoreType.DMA((before + 2,)),
+            pltpu.SemaphoreType.DMA((4,)),
+        ],
+        compiler_params=pltpu.CompilerParams(vmem_limit_bytes=20 * MIB),
         cost_estimate=pl.CostEstimate(flops=4_200_000_000, bytes_accessed=8_000_000, transcendentals=262144),
         name="attend",
     )(me, count, *normed, *proj, first, second, weights, gain, queries, d_out)
@@ -188,40 +190,40 @@
     )(at, incoming, weights, gain)
 
 
-def reduce_kernel(me_ref, in_ref, red_ref, pay_ref):
-    width = red_ref.shape[1]
-    blocks = in_ref.shape[0]
+def reduce_kernel(me_ref, in_ref, gain_ref, red_ref, pay_ref):
     total = in_ref[0].astype(f32)
-    for i in range(1, blocks):
+    for i in range(1, in_ref.shape[0]):
         total = total + in_ref[i].astype(f32)
-    red = total[:, :width]
-    red_ref[...] = red
-    squares = jnp.sum(jnp.sum(red * red, axis=1, keepdims=True), axis=0, keepdims=True)
-    gain = total[0:1, width:] + total[1:2, width:]
-    quarter = me_ref[0] % 4
-    lane = lax.broadcasted_iota(jnp.int32, (1, 128), 1)
-    gain = jnp.where(lane // 32 == quarter, gain, 0.0)
-    pay = jnp.where(lane == ((quarter + 1) % 4) * 32, squares, gain)
-    pay_ref[...] = jnp.broadcast_to(pay[None], pay_ref.shape)
-
-
-def final_kernel(pay_ref, red_ref, grad_ref, gain_ref):
-    blocks = 32
-    pay = pay_ref[...].reshape(blocks, 8, 128)
-    rows = jnp.sum(pay, axis=1)
-    row = lax.broadcasted_iota(jnp.int32, (blocks, 128), 0)
-    lane = lax.broadcasted_iota(jnp.int32, (blocks, 128), 1)
-    gains = jnp.where((lane // 32 == row % 4) & (row < 28), rows, 0.0)
-    gains = jnp.sum(gains.reshape(8, 4, 128), axis=1)
-    squares = jnp.where(lane == ((row + 1) % 4) * 32, rows, 0.0)
+    red_ref[...] = total
+    squares = jnp.sum(jnp.sum(total * total, axis=1, keepdims=True), axis=0, keepdims=True)
+    lane = lax.broadcasted_iota(jnp.int32, (8, 128), 1)
+    pay = jnp.broadcast_to(squares, (8, 128))
+    for t in range(gain_ref.shape[1] // 128):
+        tile = jnp.broadcast_to(gain_ref[:, t * 128 : (t + 1) * 128], (8, 128))
+        turn = lax.rem(16 * t + 128 - 16 * me_ref[1], 128)
+        pay = jnp.where(lane // 16 == t, pltpu.roll(tile, turn, 1), pay)
+    pay_ref[...] = jnp.broadcast_to(pay[0:1][None], pay_ref.shape)
+
+
+def final_kernel(count, pay_ref, red_ref, grad_ref, gain_ref):
+    rows = jnp.sum(pay_ref[...].reshape(-1, 8, 128), axis=0)
+    row = lax.broadcasted_iota(jnp.int32, (8, 128), 0)
+    lane = lax.broadcasted_iota(jnp.int32, (8, 128), 1)
+    turned = [rows] + [pltpu.roll(rows, 16 * d, 1) for d in range(1, 8)]
+    gains = []
+    for t in range(gain_ref.shape[0] // 128):
+        tile = jnp.zeros((8, 128), f32)
+        for d in range(8):
+            tile = jnp.where((row == lane // 16) & (row == (t + d) % 8), turned[d], tile)
+        gains.append(jnp.sum(tile, axis=0, keepdims=True))
+    squares = jnp.where(lane == 112, rows, 0.0)
+    for tile in gains:
+        squares = squares + jnp.where(row == 0, jnp.broadcast_to(tile * tile, (8, 128)), 0.0)
     total = jnp.sum(jnp.sum(squares, axis=1, keepdims=True), axis=0, keepdims=True)
-    total = total + jnp.sum(jnp.sum(gains * gains, axis=1, keepdims=True), axis=0, keepdims=True)
-    count = 4096 * 896 + 896
     factor = jnp.minimum(1.0, clip_rms * lax.rsqrt(total / count + epsilon))
     grad_ref[...] = red_ref[...] * factor
-    gains = gains * factor
-    for t in range(gain_ref.shape[0] // 128):
-        gain_ref[t * 128 : (t + 1) * 128] = gains[t]
+    for t, tile in enumerate(gains):
+        gain_ref[t * 128 : (t + 1) * 128] = (tile * factor)[0]
 
 
 def on_device(queries, d_out, database, kv_weight, gain, nbr_owner, nbr_row, nbr_count):
@@ -275,7 +277,7 @@
     pieces = [(own, other), (near, move(near, swap)), (near_b, move(near_b, swap))]
     done = [project_call(x, y, weights, gain_full, stretches) for x, y in pieces]
     far, done[0], done[1] = lax.optimization_barrier((far, done[0], done[1]))
-    att, blocks = main_call(
+    att, blocks, gain_part = main_call(
         me,
         nbr_count,
         [n for n, _ in done],
@@ -287,6 +289,8 @@
         queries,
         d_out,
     )
+    for step in (1, 2, 4):
+        gain_part = gain_part + lax.ppermute(gain_part, "fsdp", [(i, i ^ step) for i in range(shards)])
     rows_here = length // shards
     att = att.reshape(stretches, shards, rows_here, 2 * HEAD)
     attended = jnp.zeros((stretches, rows_here, head_dim), bf16)
@@ -299,7 +303,7 @@
     blocks = lax.all_to_all(blocks, "dp", split_axis=0, concat_axis=0, tiled=True)
     reduced, payload = pl.pallas_call(
         reduce_kernel,
-        in_specs=[SMEM, VMEM],
+        in_specs=[SMEM, VMEM, VMEM],
         out_specs=[VMEM] * 2,
         out_shape=[
             jax.ShapeDtypeStruct((16, width), f32),
@@ -307,7 +311,7 @@
         ],
         compiler_params=pltpu.CompilerParams(vmem_limit_bytes=4 * MIB),
         name="reduce",
-    )(me, blocks)
+    )(me, blocks, gain_part)
     pairs = []
     for p in range(groups):
         kv, odd_head, piece = p // 16, (p // 8) % 2, p % 8
@@ -316,7 +320,7 @@
     moved = lax.ppermute(reduced, ("dp", "fsdp"), pairs)
     payload = lax.all_to_all(payload, ("dp", "fsdp"), split_axis=0, concat_axis=0, tiled=True)
     kv_grad, gain_grad = pl.pallas_call(
-        final_kernel,
+        functools.partial(final_kernel, groups * 16 * shards * width + width),
         out_shape=[
             jax.ShapeDtypeStruct((16, width), f32),
             jax.ShapeDtypeStruct((width,), f32),

time: 154 us -> 150 us (0.974)
  waiting for transfers between devices: 84.4 us -> 77.1 us
  starting transfers between devices: 45.6 us -> 50.1 us
    all_to_all x1, waiting for transfers between devices: 21.3 us -> 11 us  [on_device(): lax.all_to_all(blocks, 'dp', split_axis=0, concat_axis=0, tiled=True)]
    ppermute x0 -> x3, starting transfers between devices: none -> 4.6 us  [on_device(): lax.ppermute(gain_part, 'fsdp', [(i, i ^ step) for i in range(shards)])]
    ppermute x0 -> x3, waiting for transfers between devices: none -> 3.13 us  [on_device(): lax.ppermute(gain_part, 'fsdp', [(i, i ^ step) for i in range(shards)])]
  transfers between devices with their start and end apart: 23 -> 26, of which waited for: 12 -> 13; matrix products, arithmetic and copies ran while one was open for 1% -> 1% of each run, Pallas kernels for 3% -> 3%
where the time goes in v3:
time: 150 us
  waiting for transfers between devices  77.1 us (51%)
  starting transfers between devices  50.1 us (33%)
  Pallas kernels  15.9 us (11%)
  other arithmetic  3.13 us (2%)
  local copies, waits for them, and re-layouts  2.68 us (2%)
    all_to_all x1, waiting for transfers between devices, on_device(): lax.all_to_all(outgoing.reshape(groups, capacity, per, width), 'dp', spli...  23.8 us
    ppermute x3, waiting for transfers between devices, on_device(): lax.ppermute(gain_full, 'fsdp', [(i, i ^ step) for i in range(shards)])  13.5 us
    ppermute x7, waiting for transfers between devices, on_device(): move = lambda block, pairs: lax.ppermute(block, 'fsdp', pairs)  13.1 us
    ppermute x1, waiting for transfers between devices, on_device(): moved = lax.ppermute(reduced, ('dp', 'fsdp'), pairs)  12.5 us
    all_to_all x1, starting transfers between devices, on_device(): lax.all_to_all(outgoing.reshape(groups, capacity, per, width), 'dp', spli...  11.3 us
    all_to_all x1, waiting for transfers between devices, on_device(): lax.all_to_all(blocks, 'dp', split_axis=0, concat_axis=0, tiled=True)  11 us
    pallas_call x1, Pallas kernels, main_call(): pl.pallas_call(functools.partial(main_kernel, before), in_specs=[SMEM] *...  9.65 us
    all_to_all x1, starting transfers between devices, on_device(): lax.all_to_all(payload, ('dp', 'fsdp'), split_axis=0, concat_axis=0, tile...  8.32 us
  transfers between devices with their start and end apart: 26, of which 13 were waited for; matrix products, arithmetic and copies ran while one was open for 1% of the time, Pallas kernels for 3%

profile of v3, /device:TPU:48, one launch (start us, length us, event | category | flops | bytes accessed | tf_op | source)
XLA Modules:
  0.0 150.0 jit_solution(15905101606353630741)
XLA Ops:
  2.5 2.0 %gather_fusion = bf16[64,16,896]{2,1,0:T(8,128)(2,1)} fusion(bf16[16,16,896]{2,1,0:T(8,128)(2,1)S(1)} %copy-done, s32[1024]{0:T(1024)S(1)} %pad_clamp_fusion), kind=kCustom, calls=%fused_computation | custom fusion | bytes 3670272 | tf_op jit(solution)/shard_map/jit(_take)/gather | solution.py:247
  4.5 11.3 %all-to-all-start = ((bf16[32,2,16,896]{3,2,1,0:T(8,128)(2,1)}), bf16[32,2,16,896]{3,2,1,0:T(8,128)(2,1)S(1)}, u32[]{:S(2)}, u32[]{:S(2)}) async-start(bf16[32,2,16,896]{3,2,1,0:T(8,128)(2,1)} %bitcast.32), calls=%async_computation | async-start | bytes 3670016 | tf_op jit(solution)/shard_map/all_to_all | solution.py:248
  15.9 1.0 broadcast_select_fusion.1
  17.2 2.1 %collective-permute-start.1 = (bf16[256,896]{1,0:T(8,128)(2,1)}, bf16[256,896]{1,0:T(8,128)(2,1)S(1)}, u32[]{:S(2)}, u32[]{:S(2)}) collective-permute-start(bf16[256,896]{1,0:T(8,128)(2,1)} %get-tuple-element.44), channel_id=1, source_target_pairs={{0,0},{1,2},{2,4},{3,6},{4,1},{5,3},{6,5},{7,7},{8,8},{9,10},{10,1... | collective-permute-start | bytes 1376264 | tf_op jit(solution)/shard_map/ppermute | solution.py:260
  19.4 1.0 collective-permute-start.2
  21.3 1.2 collective-permute-start.3
  22.7 7.9 %collective-permute-done.3 = bf16[1,896]{1,0:T(2,128)(2,1)S(1)} collective-permute-done((bf16[1,896]{1,0:T(2,128)(2,1)S(1)}, bf16[1,896]{1,0:T(2,128)(2,1)S(1)}, u32[]{:S(2)}, u32[]{:S(2)}) %collective-permute-start.3) | collective-permute-done | bytes 1824 | tf_op jit(solution)/shard_map/ppermute | solution.py:267
  30.7 5.1 %collective-permute-done.4 = bf16[1,896]{1,0:T(2,128)(2,1)S(1)} collective-permute-done((bf16[1,896]{1,0:T(2,128)(2,1)S(1)}, bf16[1,896]{1,0:T(2,128)(2,1)S(1)}, u32[]{:S(2)}, u32[]{:S(2)}) %collective-permute-start.4) | collective-permute-done | bytes 1824 | tf_op jit(solution)/shard_map/ppermute | solution.py:267
  36.0 23.8 %all-to-all-done = bf16[32,2,16,896]{3,2,1,0:T(8,128)(2,1)S(1)} async-done(((bf16[32,2,16,896]{3,2,1,0:T(8,128)(2,1)}), bf16[32,2,16,896]{3,2,1,0:T(8,128)(2,1)S(1)}, u32[]{:S(2)}, u32[]{:S(2)}) %all-to-all-start) | async-done | bytes 1835040 | tf_op jit(solution)/shard_map/all_to_all | solution.py:248
  59.8 1.3 pick.1.a_ref
  61.2 1.4 collective-permute-start.5
  63.0 1.3 collective-permute-start.9
  64.3 5.5 %collective-permute-done.5.a_ref = bf16[256,896]{1,0:T(8,128)(2,1)S(1)} collective-permute-done((bf16[256,896]{1,0:T(8,128)(2,1)S(1)}, bf16[256,896]{1,0:T(8,128)(2,1)S(1)}, u32[]{:S(2)}, u32[]{:S(2)}) %collective-permute-start.5) | collective-permute-done | bytes 458784 | tf_op jit(solution)/shard_map/ppermute | solution.py:272
  69.7 1.8 %collective-permute-start.6 = (bf16[256,896]{1,0:T(8,128)(2,1)S(1)}, bf16[256,896]{1,0:T(8,128)(2,1)S(1)}, u32[]{:S(2)}, u32[]{:S(2)}) collective-permute-start(bf16[256,896]{1,0:T(8,128)(2,1)S(1)} %collective-permute-done.5.a_ref), channel_id=1, source_target_pairs={{0,2},{1,7},{2,4},{3,1},{4,6},{5,3},{6,0},{7,5},{8,10},{9,15},{10,... | collective-permute-start | bytes 1376264 | tf_op jit(solution)/shard_map/ppermute | solution.py:272
  72.4 2.3 %collective-permute-done.9.a_ref = bf16[256,896]{1,0:T(8,128)(2,1)S(1)} collective-permute-done((bf16[256,896]{1,0:T(8,128)(2,1)S(1)}, bf16[256,896]{1,0:T(8,128)(2,1)S(1)}, u32[]{:S(2)}, u32[]{:S(2)}) %collective-permute-start.9) | collective-permute-done | bytes 458784 | tf_op jit(solution)/shard_map/ppermute | solution.py:272
  75.5 4.1 %collective-permute-done.6.refs_6_ = bf16[256,896]{1,0:T(8,128)(2,1)S(1)} collective-permute-done((bf16[256,896]{1,0:T(8,128)(2,1)S(1)}, bf16[256,896]{1,0:T(8,128)(2,1)S(1)}, u32[]{:S(2)}, u32[]{:S(2)}) %collective-permute-start.6) | collective-permute-done | bytes 458784 | tf_op jit(solution)/shard_map/ppermute | solution.py:272
  81.4 9.6 %attend.1 = (bf16[8,64,256]{2,1,0:T(8,128)(2,1)S(1)}, bf16[32,16,896]{2,1,0:T(8,128)(2,1)}, f32[1,896]{1,0:T(1,128)S(1)}) custom-call(s32[2]{0:T(128)S(1)} %pad_add_fusion.1.me_ref, s32[8]{0:T(128)S(1)} %copy-done.3, bf16[8,64,896]{2,1,0:T(8,128)(2,1)S(1)} %get-tuple-element.25.refs_0_, bf16[8,64,896]{2,1,0:T(8,128)(2,1)S(1)} %get-tuple-element.26.refs_1_, ...), custom_call_target="tpu_custom_call" | custom-call | flops 4200000000 | bytes 8000000 | tf_op jit(solution)/shard_map/attend/pallas_call | solution.py:142
  91.1 6.6 %all-to-all-start.1 = ((bf16[32,16,896]{2,1,0:T(8,128)(2,1)}), bf16[32,16,896]{2,1,0:T(8,128)(2,1)S(1)}, u32[]{:S(2)}, u32[]{:S(2)}) async-start(bf16[32,16,896]{2,1,0:T(8,128)(2,1)} %get-tuple-element.33), calls=%async_computation.1 | async-start | bytes 1835008 | tf_op jit(solution)/shard_map/all_to_all | solution.py:303
  97.9 1.1 collective-permute-done.19
  98.9 1.4 collective-permute-start.20
  101.2 1.2 collective-permute-start.14
  102.9 3.1 %collective-permute-start.21 = (f32[1,896]{1,0:T(1,128)S(1)}, f32[1,896]{1,0:T(1,128)S(1)}, u32[]{:S(2)}, u32[]{:S(2)}) collective-permute-start(f32[1,896]{1,0:T(1,128)S(1)} %add.163), channel_id=1, source_target_pairs={{0,4},{1,5},{2,6},{3,7},{4,0},{5,1},{6,2},{7,3},{8,12},{9,13},{10,... | collective-permute-start | bytes 10760 | tf_op jit(solution)/shard_map/ppermute | solution.py:293
  106.0 2.0 %collective-permute-done.21 = f32[1,896]{1,0:T(1,128)S(1)} collective-permute-done((f32[1,896]{1,0:T(1,128)S(1)}, f32[1,896]{1,0:T(1,128)S(1)}, u32[]{:S(2)}, u32[]{:S(2)}) %collective-permute-start.21) | collective-permute-done | bytes 3616 | tf_op jit(solution)/shard_map/ppermute | solution.py:293
  108.1 1.5 %collective-permute-start.16 = (bf16[8,8,256]{2,1,0:T(8,128)(2,1)S(1)}, bf16[8,8,256]{2,1,0:T(8,128)(2,1)S(1)}, u32[]{:S(2)}, u32[]{:S(2)}) collective-permute-start(bf16[8,8,256]{2,1,0:T(8,128)(2,1)S(1)} %get-tuple-element.47), channel_id=1, source_target_pairs={{0,5},{1,4},{2,7},{3,6},{4,1},{5,0},{6,3},{7,2},{8,13},{9,12},{10,... | collective-permute-start | bytes 98312 | tf_op jit(solution)/shard_map/ppermute | solution.py:301
  109.6 1.1 collective-permute-start.17
  110.8 2.0 %collective-permute-start.18 = (bf16[8,8,256]{2,1,0:T(8,128)(2,1)S(1)}, bf16[8,8,256]{2,1,0:T(8,128)(2,1)S(1)}, u32[]{:S(2)}, u32[]{:S(2)}) collective-permute-start(bf16[8,8,256]{2,1,0:T(8,128)(2,1)S(1)} %get-tuple-element.45), channel_id=1, source_target_pairs={{0,7},{1,6},{2,5},{3,4},{4,3},{5,2},{6,1},{7,0},{8,15},{9,14},{10,... | collective-permute-start | bytes 98312 | tf_op jit(solution)/shard_map/ppermute | solution.py:301
  112.8 11.0 %all-to-all-done.1.in_ref = bf16[32,16,896]{2,1,0:T(8,128)(2,1)S(1)} async-done(((bf16[32,16,896]{2,1,0:T(8,128)(2,1)}), bf16[32,16,896]{2,1,0:T(8,128)(2,1)S(1)}, u32[]{:S(2)}, u32[]{:S(2)}) %all-to-all-start.1) | async-done | bytes 917536 | tf_op jit(solution)/shard_map/all_to_all | solution.py:303
  123.8 1.5 reduce.1
  125.3 8.3 %all-to-all-start.2 = ((f32[256,1,128]{2,1,0:T(1,128)}), f32[256,1,128]{2,1,0:T(1,128)S(1)}, u32[]{:S(2)}, u32[]{:S(2)}) async-start(f32[256,1,128]{2,1,0:T(1,128)} %get-tuple-element.35), calls=%async_computation.2 | async-start | bytes 262144 | tf_op jit(solution)/shard_map/all_to_all | solution.py:321
  133.7 2.9 %collective-permute-start.22 = (f32[16,896]{1,0:T(8,128)S(1)}, f32[16,896]{1,0:T(8,128)S(1)}, u32[]{:S(2)}, u32[]{:S(2)}) collective-permute-start(f32[16,896]{1,0:T(8,128)S(1)} %get-tuple-element.36), channel_id=1, source_target_pairs={{0,0},{1,16},{2,32},{3,48},{4,64},{5,80},{6,96},{7,112},{8,1},{9,1... | collective-permute-start | bytes 172040 | tf_op jit(solution)/shard_map/ppermute | solution.py:320
  136.6 12.5 %collective-permute-done.22.red_ref = f32[16,896]{1,0:T(8,128)S(1)} collective-permute-done((f32[16,896]{1,0:T(8,128)S(1)}, f32[16,896]{1,0:T(8,128)S(1)}, u32[]{:S(2)}, u32[]{:S(2)}) %collective-permute-start.22) | collective-permute-done | bytes 57376 | tf_op jit(solution)/shard_map/ppermute | solution.py:320
  149.1 0.9 finish.1
  (83 shorter events, 9.2 us)
Async XLA Ops:
  4.5 11.4 %copy-start.4 = (bf16[512,896]{1,0:T(8,128)(2,1)S(1)}, bf16[512,896]{1,0:T(8,128)(2,1)}, u32[]{:S(2)}) copy-start(bf16[512,896]{1,0:T(8,128)(2,1)} %param.11) | copy-start | bytes 2752516
  4.5 55.3 %all-to-all-start = ((bf16[32,2,16,896]{3,2,1,0:T(8,128)(2,1)}), bf16[32,2,16,896]{3,2,1,0:T(8,128)(2,1)S(1)}, u32[]{:S(2)}, u32[]{:S(2)}) async-start(bf16[32,2,16,896]{3,2,1,0:T(8,128)(2,1)} %bitcast.32), calls=%async_computation | async-start | bytes 3670016 | tf_op jit(solution)/shard_map/all_to_all | solution.py:248
  15.8 4.6 %copy-start.6 = (s32[256,2]{0,1:T(2,128)S(1)}, s32[256,2]{0,1:T(2,128)}, u32[]{:S(2)}) copy-start(s32[256,2]{0,1:T(2,128)} %param.13) | copy-start | bytes 6148
  16.9 18.9 %collective-permute-start = (bf16[256,896]{1,0:T(8,128)(2,1)}, bf16[256,896]{1,0:T(8,128)(2,1)S(1)}, u32[]{:S(2)}, u32[]{:S(2)}) collective-permute-start(bf16[256,896]{1,0:T(8,128)(2,1)} %get-tuple-element.43), channel_id=1, source_target_pairs={{0,1},{1,3},{2,5},{3,7},{4,0},{5,2},{6,4},{7,6},{8,9},{9,11},{10,1... | collective-permute-start | bytes 1376264 | tf_op jit(solution)/shard_map/ppermute | solution.py:261
  17.2 18.6 %collective-permute-start.1 = (bf16[256,896]{1,0:T(8,128)(2,1)}, bf16[256,896]{1,0:T(8,128)(2,1)S(1)}, u32[]{:S(2)}, u32[]{:S(2)}) collective-permute-start(bf16[256,896]{1,0:T(8,128)(2,1)} %get-tuple-element.44), channel_id=1, source_target_pairs={{0,0},{1,2},{2,4},{3,6},{4,1},{5,3},{6,5},{7,7},{8,8},{9,10},{10,1... | collective-permute-start | bytes 1376264 | tf_op jit(solution)/shard_map/ppermute | solution.py:260
  19.4 1.9 %collective-permute-start.2 = (bf16[1,896]{1,0:T(2,128)(2,1)S(1)}, bf16[1,896]{1,0:T(2,128)(2,1)S(1)}, u32[]{:S(2)}, u32[]{:S(2)}) collective-permute-start(bf16[1,896]{1,0:T(2,128)(2,1)S(1)} %compare_select_fusion), channel_id=1, source_target_pairs={{0,1},{1,0},{2,3},{3,2},{4,5},{5,4},{6,7},{7,6},{8,9},{9,8},{10,11... | collective-permute-start | bytes 5384 | tf_op jit(solution)/shard_map/ppermute | solution.py:267
  21.3 9.2 %collective-permute-start.3 = (bf16[1,896]{1,0:T(2,128)(2,1)S(1)}, bf16[1,896]{1,0:T(2,128)(2,1)S(1)}, u32[]{:S(2)}, u32[]{:S(2)}) collective-permute-start(bf16[1,896]{1,0:T(2,128)(2,1)S(1)} %fusion.8), channel_id=1, source_target_pairs={{0,2},{1,3},{2,0},{3,1},{4,6},{5,7},{6,4},{7,5},{8,10},{9,11},{10,... | collective-permute-start | bytes 5384 | tf_op jit(solution)/shard_map/ppermute | solution.py:267
  30.6 5.2 %collective-permute-start.4 = (bf16[1,896]{1,0:T(2,128)(2,1)S(1)}, bf16[1,896]{1,0:T(2,128)(2,1)S(1)}, u32[]{:S(2)}, u32[]{:S(2)}) collective-permute-start(bf16[1,896]{1,0:T(2,128)(2,1)S(1)} %add.144), channel_id=1, source_target_pairs={{0,4},{1,5},{2,6},{3,7},{4,0},{5,1},{6,2},{7,3},{8,12},{9,13},{10,... | collective-permute-start | bytes 5384 | tf_op jit(solution)/shard_map/ppermute | solution.py:267
  61.1 1.9 %collective-permute-start.7 = (bf16[256,896]{1,0:T(8,128)(2,1)S(1)}, bf16[256,896]{1,0:T(8,128)(2,1)S(1)}, u32[]{:S(2)}, u32[]{:S(2)}) collective-permute-start(bf16[256,896]{1,0:T(8,128)(2,1)S(1)} %pick.1.a_ref), channel_id=1, source_target_pairs={{0,1},{1,0},{2,3},{3,2},{4,5},{5,4},{6,7},{7,6},{8,9},{9,8},{10,11... | collective-permute-start | bytes 1376264 | tf_op jit(solution)/shard_map/ppermute | solution.py:272
  61.2 8.6 %collective-permute-start.5 = (bf16[256,896]{1,0:T(8,128)(2,1)S(1)}, bf16[256,896]{1,0:T(8,128)(2,1)S(1)}, u32[]{:S(2)}, u32[]{:S(2)}) collective-permute-start(bf16[256,896]{1,0:T(8,128)(2,1)S(1)} %pick.1.a_ref), channel_id=1, source_target_pairs={{0,2},{1,7},{2,4},{3,1},{4,6},{5,3},{6,0},{7,5},{8,10},{9,15},{10,... | collective-permute-start | bytes 1376264 | tf_op jit(solution)/shard_map/ppermute | solution.py:272
  63.0 11.7 %collective-permute-start.9 = (bf16[256,896]{1,0:T(8,128)(2,1)S(1)}, bf16[256,896]{1,0:T(8,128)(2,1)S(1)}, u32[]{:S(2)}, u32[]{:S(2)}) collective-permute-start(bf16[256,896]{1,0:T(8,128)(2,1)S(1)} %collective-permute-done.7.b_ref), channel_id=1, source_target_pairs={{0,2},{1,7},{2,4},{3,1},{4,6},{5,3},{6,0},{7,5},{8,10},{9,15},{10,... | collective-permute-start | bytes 1376264 | tf_op jit(solution)/shard_map/ppermute | solution.py:272
  69.7 4.9 %collective-permute-start.8 = (bf16[256,896]{1,0:T(8,128)(2,1)S(1)}, bf16[256,896]{1,0:T(8,128)(2,1)S(1)}, u32[]{:S(2)}, u32[]{:S(2)}) collective-permute-start(bf16[256,896]{1,0:T(8,128)(2,1)S(1)} %collective-permute-done.5.a_ref), channel_id=1, source_target_pairs={{0,1},{1,0},{2,3},{3,2},{4,5},{5,4},{6,7},{7,6},{8,9},{9,8},{10,11... | collective-permute-start | bytes 1376264 | tf_op jit(solution)/shard_map/ppermute | solution.py:272
  69.7 9.8 %collective-permute-start.6 = (bf16[256,896]{1,0:T(8,128)(2,1)S(1)}, bf16[256,896]{1,0:T(8,128)(2,1)S(1)}, u32[]{:S(2)}, u32[]{:S(2)}) collective-permute-start(bf16[256,896]{1,0:T(8,128)(2,1)S(1)} %collective-permute-done.5.a_ref), channel_id=1, source_target_pairs={{0,2},{1,7},{2,4},{3,1},{4,6},{5,3},{6,0},{7,5},{8,10},{9,15},{10,... | collective-permute-start | bytes 1376264 | tf_op jit(solution)/shard_map/ppermute | solution.py:272
  71.5 9.9 %copy-start.2 = (bf16[8,64,2048]{2,1,0:T(8,128)(2,1)S(1)}, bf16[8,64,2048]{2,1,0:T(8,128)(2,1)}, u32[]{:S(2)}) copy-start(bf16[8,64,2048]{2,1,0:T(8,128)(2,1)} %refs_11_.1) | copy-start | bytes 6291460
  72.4 9.0 %copy-start.1 = (bf16[8,64,2048]{2,1,0:T(8,128)(2,1)S(1)}, bf16[8,64,2048]{2,1,0:T(8,128)(2,1)}, u32[]{:S(2)}) copy-start(bf16[8,64,2048]{2,1,0:T(8,128)(2,1)} %refs_10_.1) | copy-start | bytes 6291460
  72.4 9.0 %copy-start.3 = (s32[8]{0:T(128)S(1)}, s32[8]{0:T(128)}, u32[]{:S(2)}) copy-start(s32[8]{0:T(128)} %count_ref.1) | copy-start | bytes 100
  74.7 5.0 %collective-permute-start.10 = (bf16[256,896]{1,0:T(8,128)(2,1)S(1)}, bf16[256,896]{1,0:T(8,128)(2,1)S(1)}, u32[]{:S(2)}, u32[]{:S(2)}) collective-permute-start(bf16[256,896]{1,0:T(8,128)(2,1)S(1)} %collective-permute-done.9.a_ref), channel_id=1, source_target_pairs={{0,1},{1,0},{2,3},{3,2},{4,5},{5,4},{6,7},{7,6},{8,9},{9,8},{10,11... | collective-permute-start | bytes 1376264 | tf_op jit(solution)/shard_map/ppermute | solution.py:272
  79.6 1.8 %collective-permute-start.11 = (bf16[256,896]{1,0:T(8,128)(2,1)S(1)}, bf16[256,896]{1,0:T(8,128)(2,1)S(1)}, u32[]{:S(2)}, u32[]{:S(2)}) collective-permute-start(bf16[256,896]{1,0:T(8,128)(2,1)S(1)} %collective-permute-done.6.refs_6_), channel_id=1, source_target_pairs={{0,1},{1,0},{2,3},{3,2},{4,5},{5,4},{6,7},{7,6},{8,9},{9,8},{10,11... | collective-permute-start | bytes 1376264 | tf_op jit(solution)/shard_map/ppermute | solution.py:272
  91.1 32.8 %all-to-all-start.1 = ((bf16[32,16,896]{2,1,0:T(8,128)(2,1)}), bf16[32,16,896]{2,1,0:T(8,128)(2,1)S(1)}, u32[]{:S(2)}, u32[]{:S(2)}) async-start(bf16[32,16,896]{2,1,0:T(8,128)(2,1)} %get-tuple-element.33), calls=%async_computation.1 | async-start | bytes 1835008 | tf_op jit(solution)/shard_map/all_to_all | solution.py:303
  97.7 1.3 collective-permute-start.19
  98.9 3.9 %collective-permute-start.20 = (f32[1,896]{1,0:T(1,128)S(1)}, f32[1,896]{1,0:T(1,128)S(1)}, u32[]{:S(2)}, u32[]{:S(2)}) collective-permute-start(f32[1,896]{1,0:T(1,128)S(1)} %add.162), channel_id=1, source_target_pairs={{0,2},{1,3},{2,0},{3,1},{4,6},{5,7},{6,4},{7,5},{8,10},{9,11},{10,... | collective-permute-start | bytes 10760 | tf_op jit(solution)/shard_map/ppermute | solution.py:293
  100.4 9.3 %collective-permute-start.12 = (bf16[8,8,256]{2,1,0:T(8,128)(2,1)S(1)}, bf16[8,8,256]{2,1,0:T(8,128)(2,1)S(1)}, u32[]{:S(2)}, u32[]{:S(2)}) collective-permute-start(bf16[8,8,256]{2,1,0:T(8,128)(2,1)S(1)} %get-tuple-element.51), channel_id=1, source_target_pairs={{0,1},{1,0},{2,3},{3,2},{4,5},{5,4},{6,7},{7,6},{8,9},{9,8},{10,11... | collective-permute-start | bytes 98312 | tf_op jit(solution)/shard_map/ppermute | solution.py:301
  100.5 10.3 %collective-permute-start.13 = (bf16[8,8,256]{2,1,0:T(8,128)(2,1)S(1)}, bf16[8,8,256]{2,1,0:T(8,128)(2,1)S(1)}, u32[]{:S(2)}, u32[]{:S(2)}) collective-permute-start(bf16[8,8,256]{2,1,0:T(8,128)(2,1)S(1)} %get-tuple-element.50), channel_id=1, source_target_pairs={{0,2},{1,3},{2,0},{3,1},{4,6},{5,7},{6,4},{7,5},{8,10},{9,11},{10,... | collective-permute-start | bytes 98312 | tf_op jit(solution)/shard_map/ppermute | solution.py:301
  101.2 11.6 %collective-permute-start.14 = (bf16[8,8,256]{2,1,0:T(8,128)(2,1)S(1)}, bf16[8,8,256]{2,1,0:T(8,128)(2,1)S(1)}, u32[]{:S(2)}, u32[]{:S(2)}) collective-permute-start(bf16[8,8,256]{2,1,0:T(8,128)(2,1)S(1)} %get-tuple-element.49), channel_id=1, source_target_pairs={{0,3},{1,2},{2,1},{3,0},{4,7},{5,6},{6,5},{7,4},{8,11},{9,10},{10,... | collective-permute-start | bytes 98312 | tf_op jit(solution)/shard_map/ppermute | solution.py:301
  102.4 10.4 %collective-permute-start.15 = (bf16[8,8,256]{2,1,0:T(8,128)(2,1)S(1)}, bf16[8,8,256]{2,1,0:T(8,128)(2,1)S(1)}, u32[]{:S(2)}, u32[]{:S(2)}) collective-permute-start(bf16[8,8,256]{2,1,0:T(8,128)(2,1)S(1)} %get-tuple-element.48), channel_id=1, source_target_pairs={{0,4},{1,5},{2,6},{3,7},{4,0},{5,1},{6,2},{7,3},{8,12},{9,13},{10,... | collective-permute-start | bytes 98312 | tf_op jit(solution)/shard_map/ppermute | solution.py:301
  102.9 5.2 %collective-permute-start.21 = (f32[1,896]{1,0:T(1,128)S(1)}, f32[1,896]{1,0:T(1,128)S(1)}, u32[]{:S(2)}, u32[]{:S(2)}) collective-permute-start(f32[1,896]{1,0:T(1,128)S(1)} %add.163), channel_id=1, source_target_pairs={{0,4},{1,5},{2,6},{3,7},{4,0},{5,1},{6,2},{7,3},{8,12},{9,13},{10,... | collective-permute-start | bytes 10760 | tf_op jit(solution)/shard_map/ppermute | solution.py:293
  108.1 25.5 %collective-permute-start.16 = (bf16[8,8,256]{2,1,0:T(8,128)(2,1)S(1)}, bf16[8,8,256]{2,1,0:T(8,128)(2,1)S(1)}, u32[]{:S(2)}, u32[]{:S(2)}) collective-permute-start(bf16[8,8,256]{2,1,0:T(8,128)(2,1)S(1)} %get-tuple-element.47), channel_id=1, source_target_pairs={{0,5},{1,4},{2,7},{3,6},{4,1},{5,0},{6,3},{7,2},{8,13},{9,12},{10,... | collective-permute-start | bytes 98312 | tf_op jit(solution)/shard_map/ppermute | solution.py:301
  109.6 24.0 %collective-permute-start.17 = (bf16[8,8,256]{2,1,0:T(8,128)(2,1)S(1)}, bf16[8,8,256]{2,1,0:T(8,128)(2,1)S(1)}, u32[]{:S(2)}, u32[]{:S(2)}) collective-permute-start(bf16[8,8,256]{2,1,0:T(8,128)(2,1)S(1)} %get-tuple-element.46), channel_id=1, source_target_pairs={{0,6},{1,7},{2,4},{3,5},{4,2},{5,3},{6,0},{7,1},{8,14},{9,15},{10,... | collective-permute-start | bytes 98312 | tf_op jit(solution)/shard_map/ppermute | solution.py:301
  110.8 25.8 %collective-permute-start.18 = (bf16[8,8,256]{2,1,0:T(8,128)(2,1)S(1)}, bf16[8,8,256]{2,1,0:T(8,128)(2,1)S(1)}, u32[]{:S(2)}, u32[]{:S(2)}) collective-permute-start(bf16[8,8,256]{2,1,0:T(8,128)(2,1)S(1)} %get-tuple-element.45), channel_id=1, source_target_pairs={{0,7},{1,6},{2,5},{3,4},{4,3},{5,2},{6,1},{7,0},{8,15},{9,14},{10,... | collective-permute-start | bytes 98312 | tf_op jit(solution)/shard_map/ppermute | solution.py:301
  125.3 23.8 %all-to-all-start.2 = ((f32[256,1,128]{2,1,0:T(1,128)}), f32[256,1,128]{2,1,0:T(1,128)S(1)}, u32[]{:S(2)}, u32[]{:S(2)}) async-start(f32[256,1,128]{2,1,0:T(1,128)} %get-tuple-element.35), calls=%async_computation.2 | async-start | bytes 262144 | tf_op jit(solution)/shard_map/all_to_all | solution.py:321
  133.7 15.4 %collective-permute-start.22 = (f32[16,896]{1,0:T(8,128)S(1)}, f32[16,896]{1,0:T(8,128)S(1)}, u32[]{:S(2)}, u32[]{:S(2)}) collective-permute-start(f32[16,896]{1,0:T(8,128)S(1)} %get-tuple-element.36), channel_id=1, source_target_pairs={{0,0},{1,16},{2,32},{3,48},{4,64},{5,80},{6,96},{7,112},{8,1},{9,1... | collective-permute-start | bytes 172040 | tf_op jit(solution)/shard_map/ppermute | solution.py:320
  136.6 13.5 %copy-start.5 = (bf16[8,8,2048]{2,1,0:T(8,128)(2,1)}, bf16[8,8,2048]{2,1,0:T(8,128)(2,1)S(1)}, u32[]{:S(2)}) copy-start(bf16[8,8,2048]{2,1,0:T(8,128)(2,1)S(1)} %constant_dynamic-update-slice_fusion) | copy-start | bytes 786436
  (2 other events, 5.3 us)

commit v4 on v3

--- a/solution.py
+++ b/solution.py
@@ -61,8 +61,8 @@
 def main_kernel(blocks_before, me_ref, count_ref, *refs):
     normed_in, refs = refs[:blocks_before], refs[blocks_before:]
     proj_in, refs = refs[:blocks_before], refs[blocks_before:]
-    a_ref, b_ref, w_ref, gain_ref, q_hbm, do_hbm, att_ref, out_ref, part_ref, *refs = refs
-    q_ref, do_ref, normed_ref, proj_ref, grad_ref, stage_ref, in_sems, out_sems = refs
+    a_ref, b_ref, w_ref, gain_ref, q_hbm, do_hbm, att_ref, keep_ref, send_ref, part_ref, *refs = refs
+    q_ref, do_ref, normed_ref, proj_ref, grad_ref, in_sems = refs
     stretches, keys, width = normed_ref.shape
     scale = HEAD ** (-0.5)
     part = normed_in[0].shape[1]
@@ -116,19 +116,14 @@
         copy.wait()
     gain_part = jnp.zeros((1, width), f32)
     normed_all = normed_ref[...].reshape(stretches * keys, width)
-    sends = []
-    for a in range(4):
-        here = slice(a * HEAD, (a + 1) * HEAD)
-        raw = dot(grad_ref[here, :], normed_all, 1, 0)
-        stage_ref[a] = raw.reshape(8, 16, width).astype(bf16)
-        sends.append(
-            pltpu.make_async_copy(stage_ref.at[a], out_ref.at[pl.ds(a * 8, 8)], out_sems.at[a])
-        )
-        sends[a].start()
-        gain_part = gain_part + jnp.sum(raw * w_ref[here, :].astype(f32), axis=0, keepdims=True)
+    odd = lax.rem(me_ref[0] // 8, 2)
+    for i in range(4):
+        at = pl.multiple_of(((i // 2 + odd) % 2 * 2 + i % 2) * HEAD, HEAD)
+        raw = dot(grad_ref[pl.ds(at, HEAD), :], normed_all, 1, 0)
+        out_ref = keep_ref if i < 2 else send_ref
+        out_ref[i % 2 * 8 : (i % 2 + 1) * 8] = raw.reshape(8, 16, width).astype(bf16)
+        gain_part = gain_part + jnp.sum(raw * w_ref[pl.ds(at, HEAD), :].astype(f32), axis=0, keepdims=True)
     part_ref[...] = gain_part / gain
-    for send in sends:
-        send.wait()
 
 
 def main_call(me, count, normed, proj, first, second, weights, gain, queries, d_out):
@@ -142,10 +137,11 @@
     return pl.pallas_call(
         functools.partial(main_kernel, before),
         in_specs=[SMEM] * 2 + [ANY] * before + [VMEM] * (before + 4) + [ANY] * 2,
-        out_specs=[VMEM, pl.BlockSpec(memory_space=pltpu.HBM), VMEM],
+        out_specs=[VMEM] * 4,
         out_shape=[
             jax.ShapeDtypeStruct((stretches, length, pair), bf16),
-            jax.ShapeDtypeStruct((blocks, 16, width), bf16),
+            jax.ShapeDtypeStruct((blocks // 2, 16, width), bf16),
+            jax.ShapeDtypeStruct((blocks // 2, 16, width), bf16),
             jax.ShapeDtypeStruct((1, width), f32),
         ],
         scratch_shapes=[
@@ -154,14 +150,45 @@
             pltpu.VMEM((stretches, keys, width), bf16),
             pltpu.VMEM((stretches, part, rows), bf16),
             pltpu.VMEM((rows, stretches * keys), bf16),
-            pltpu.VMEM((4, 8, 16, width), bf16),
             pltpu.SemaphoreType.DMA((before + 2,)),
-            pltpu.SemaphoreType.DMA((4,)),
         ],
         compiler_params=pltpu.CompilerParams(vmem_limit_bytes=20 * MIB),
         cost_estimate=pl.CostEstimate(flops=4_200_000_000, bytes_accessed=8_000_000, transcendentals=262144),
         name="attend",
     )(me, count, *normed, *proj, first, second, weights, gain, queries, d_out)
+
+
+def wanted_kernel(me_ref, owner_ref, row_ref, out_ref):
+    stretches = 8
+    shape = owner_ref.shape
+    lane = lax.broadcasted_iota(jnp.int32, shape, 1)
+    which = lax.broadcasted_iota(jnp.int32, shape, 0)
+    key = ((lane % stretches) * 2 + which) * 16 + row_ref[...]
+    mine = owner_ref[...] == me_ref[0]
+    low = jnp.where(mine, key, 256)
+    high = jnp.where(mine, key, 0)
+    low = jnp.minimum(low[0:1], low[1:2])
+    high = jnp.maximum(high[0:1], high[1:2])
+    for step in (1, 2, 4):
+        low = jnp.minimum(low, pltpu.roll(low, shape[1] - step, 1))
+        high = jnp.maximum(high, pltpu.roll(high, shape[1] - step, 1))
+    both = jnp.concatenate([low % 16, high % 16], axis=0).astype(f32)
+    source = lax.broadcasted_iota(jnp.int32, (shape[1], 128), 0)
+    slot = lax.broadcasted_iota(jnp.int32, (shape[1], 128), 1)
+    chosen = dot(both, (source == slot // 2 * stretches).astype(f32), 1, 0)
+    slot = lax.broadcasted_iota(jnp.int32, (1, 128), 1)
+    out_ref[...] = jnp.where(slot % 2 == 0, chosen[0:1], chosen[1:2]).astype(jnp.int32)
+
+
+def wanted_call(me, owner, row):
+    return pl.pallas_call(
+        wanted_kernel,
+        in_specs=[SMEM, VMEM, VMEM],
+        out_specs=VMEM,
+        out_shape=jax.ShapeDtypeStruct((1, 128), jnp.int32),
+        compiler_params=pltpu.CompilerParams(vmem_limit_bytes=4 * MIB),
+        name="wanted",
+    )(me, owner, row)
 
 
 def pick_kernel(at_ref, in_ref, w_ref, gain_ref, out_ref, sems):
@@ -188,6 +215,11 @@
         compiler_params=pltpu.CompilerParams(vmem_limit_bytes=4 * MIB),
         name="pick",
     )(at, incoming, weights, gain)
+
+
+def add_kernel(a_ref, b_ref, out_ref):
+    for i in range(out_ref.shape[0]):
+        out_ref[i] = (a_ref[i].astype(f32) + b_ref[i].astype(f32)).astype(bf16)
 
 
 def reduce_kernel(me_ref, in_ref, gain_ref, red_ref, pay_ref):
@@ -236,15 +268,8 @@
     per, width = database.shape[1:]
     entries = 2 * stretches
     capacity = 2
-    at_group = jnp.arange(groups * stretches) // stretches
-    place = jnp.arange(groups * stretches) % stretches * 2
-    order = jnp.stack([place, place + 1])
-    keys = order * 16 + nbr_row.T
-    wanted = (nbr_owner.T == group)[None] & (at_group[None, None] == jnp.arange(groups)[:, None, None])
-    first = jnp.min(jnp.where(wanted, keys[None], 256), axis=(1, 2))
-    last = jnp.max(jnp.where(wanted, keys[None], 0), axis=(1, 2))
-    picked = jnp.stack([first, last], axis=1) % 16
-    outgoing = jnp.take(database, picked.reshape(-1), axis=0, mode="clip")
+    picked = wanted_call(me, nbr_owner.T, nbr_row.T)[0, : groups * capacity]
+    outgoing = jnp.take(database, picked, axis=0, mode="clip")
     incoming = lax.all_to_all(
         outgoing.reshape(groups, capacity, per, width), "dp", split_axis=0, concat_axis=0, tiled=True
     )
@@ -277,7 +302,7 @@
     pieces = [(own, other), (near, move(near, swap)), (near_b, move(near_b, swap))]
     done = [project_call(x, y, weights, gain_full, stretches) for x, y in pieces]
     far, done[0], done[1] = lax.optimization_barrier((far, done[0], done[1]))
-    att, blocks, gain_part = main_call(
+    att, keep, send, gain_part = main_call(
         me,
         nbr_count,
         [n for n, _ in done],
@@ -300,7 +325,26 @@
         if step:
             piece = lax.ppermute(piece, "fsdp", [(i, i ^ step) for i in range(shards)])
         attended = lax.dynamic_update_slice_in_dim(attended, piece, peer * 2 * HEAD, 2)
-    blocks = lax.all_to_all(blocks, "dp", split_axis=0, concat_axis=0, tiled=True)
+    depth = 8
+    line = groups // depth
+    mates = []
+    for p in range(groups):
+        for i in range(shards):
+            x, z = p // depth, p % depth
+            mate = x ^ 1 if i % 2 == 0 else (x - 1) % line if x % 2 == 0 else (x + 1) % line
+            mates.append((p * shards + i, (mate * depth + z) * shards + i))
+    got = lax.ppermute(send, ("dp", "fsdp"), mates)
+    got, gain_part = lax.optimization_barrier((got, gain_part))
+    blocks = pl.pallas_call(
+        add_kernel,
+        in_specs=[VMEM] * 2,
+        out_specs=VMEM,
+        out_shape=jax.ShapeDtypeStruct(keep.shape, bf16),
+        compiler_params=pltpu.CompilerParams(vmem_limit_bytes=4 * MIB),
+        name="pairs",
+    )(keep, got)
+    same = [[x * depth + z for x in range(odd, line, 2) for z in range(depth)] for odd in range(2)]
+    blocks = lax.all_to_all(blocks, "dp", 0, 0, tiled=True, axis_index_groups=same)
     reduced, payload = pl.pallas_call(
         reduce_kernel,
         in_specs=[SMEM, VMEM, VMEM],
@@ -314,7 +358,7 @@
     )(me, blocks, gain_part)
     pairs = []
     for p in range(groups):
-        kv, odd_head, piece = p // 16, (p // 8) % 2, p % 8
+        odd_head, kv, piece = p // 16, (p // 8) % 2, p % 8
         for s in range(shards):
             pairs.append((p * shards + s, (kv * 16 + 2 * s + odd_head) * shards + piece))
     moved = lax.ppermute(reduced, ("dp", "fsdp"), pairs)

time: 150 us -> 151 us (level)
  other arithmetic: 3.13 us -> 1.55 us
    all_to_all x1, waiting for transfers between devices: 11 us -> 6.31 us  [on_device(): lax.all_to_all(blocks, 'dp', 0, 0, tiled=True, axis_index_groups=same)]
    ppermute x3, waiting for transfers between devices: 3.13 us -> 6.94 us  [on_device(): lax.ppermute(gain_part, 'fsdp', [(i, i ^ step) for i in range(shards)])]
    pallas_call x0 -> x2, Pallas kernels: none -> 1.78 us  [the longest x1 0.9 us: wanted_call(): pl.pallas_call(wanted_kernel, in_specs=[SMEM, VMEM, VMEM], out_specs=VMEM...]
    ppermute x3, starting transfers between devices: 4.6 us -> 2.93 us  [on_device(): lax.ppermute(gain_part, 'fsdp', [(i, i ^ step) for i in range(shards)])]
  transfers between devices with their start and end apart: 26 -> 27, of which waited for: 13 -> 15; matrix products, arithmetic and copies ran while one was open for 1% -> 1% of each run, Pallas kernels for 3% -> 3%
where the time goes in v4:
time: 151 us
  waiting for transfers between devices  77.9 us (52%)
  starting transfers between devices  49.4 us (33%)
  Pallas kernels  17 us (11%)
  local copies, waits for them, and re-layouts  3.93 us (3%)
  other arithmetic  1.55 us (1%)
    all_to_all x1, waiting for transfers between devices, on_device(): lax.all_to_all(outgoing.reshape(groups, capacity, per, width), 'dp', spli...  23.7 us
    ppermute x1, waiting for transfers between devices, on_device(): moved = lax.ppermute(reduced, ('dp', 'fsdp'), pairs)  14 us
    ppermute x3, waiting for transfers between devices, on_device(): lax.ppermute(gain_full, 'fsdp', [(i, i ^ step) for i in range(shards)])  13.5 us
    ppermute x7, waiting for transfers between devices, on_device(): move = lambda block, pairs: lax.ppermute(block, 'fsdp', pairs)  13.2 us
    all_to_all x1, starting transfers between devices, on_device(): lax.all_to_all(outgoing.reshape(groups, capacity, per, width), 'dp', spli...  11.3 us
    pallas_call x1, Pallas kernels, main_call(): pl.pallas_call(functools.partial(main_kernel, before), in_specs=[SMEM] *...  9 us
    all_to_all x1, starting transfers between devices, on_device(): lax.all_to_all(payload, ('dp', 'fsdp'), split_axis=0, concat_axis=0, tile...  8.59 us
    ppermute x7, starting transfers between devices, on_device(): piece = lax.ppermute(piece, 'fsdp', [(i, i ^ step) for i in range(shards)])  7.14 us
  transfers between devices with their start and end apart: 27, of which 15 were waited for; matrix products, arithmetic and copies ran while one was open for 1% of the time, Pallas kernels for 3%

profile of v4, /device:TPU:48, one launch (start us, length us, event | category | flops | bytes accessed | tf_op | source)
XLA Modules:
  0.0 150.9 jit_solution(2577190516715890773)
XLA Ops:
  3.1 2.0 %gather_fusion = bf16[64,16,896]{2,1,0:T(8,128)(2,1)} fusion(bf16[16,16,896]{2,1,0:T(8,128)(2,1)S(1)} %copy-done, s32[1024]{0:T(1024)S(1)} %pad_clamp_fusion), kind=kCustom, calls=%fused_computation | custom fusion | bytes 3670272 | tf_op jit(solution)/shard_map/jit(_take)/gather | solution.py:272
  5.1 11.3 %all-to-all-start = ((bf16[32,2,16,896]{3,2,1,0:T(8,128)(2,1)}), bf16[32,2,16,896]{3,2,1,0:T(8,128)(2,1)S(1)}, u32[]{:S(2)}, u32[]{:S(2)}) async-start(bf16[32,2,16,896]{3,2,1,0:T(8,128)(2,1)} %bitcast.30), calls=%async_computation | async-start | bytes 3670016 | tf_op jit(solution)/shard_map/all_to_all | solution.py:273
  16.5 1.0 broadcast_select_fusion.1
  17.8 2.1 %collective-permute-start.1 = (bf16[256,896]{1,0:T(8,128)(2,1)}, bf16[256,896]{1,0:T(8,128)(2,1)S(1)}, u32[]{:S(2)}, u32[]{:S(2)}) collective-permute-start(bf16[256,896]{1,0:T(8,128)(2,1)} %get-tuple-element.48), channel_id=1, source_target_pairs={{0,0},{1,2},{2,4},{3,6},{4,1},{5,3},{6,5},{7,7},{8,8},{9,10},{10,1... | collective-permute-start | bytes 1376264 | tf_op jit(solution)/shard_map/ppermute | solution.py:285
  21.9 1.2 collective-permute-start.3
  23.3 7.9 %collective-permute-done.3 = bf16[1,896]{1,0:T(2,128)(2,1)S(1)} collective-permute-done((bf16[1,896]{1,0:T(2,128)(2,1)S(1)}, bf16[1,896]{1,0:T(2,128)(2,1)S(1)}, u32[]{:S(2)}, u32[]{:S(2)}) %collective-permute-start.3) | collective-permute-done | bytes 1824 | tf_op jit(solution)/shard_map/ppermute | solution.py:292
  31.3 5.1 %collective-permute-done.4 = bf16[1,896]{1,0:T(2,128)(2,1)S(1)} collective-permute-done((bf16[1,896]{1,0:T(2,128)(2,1)S(1)}, bf16[1,896]{1,0:T(2,128)(2,1)S(1)}, u32[]{:S(2)}, u32[]{:S(2)}) %collective-permute-start.4) | collective-permute-done | bytes 1824 | tf_op jit(solution)/shard_map/ppermute | solution.py:292
  36.6 23.7 %all-to-all-done = bf16[32,2,16,896]{3,2,1,0:T(8,128)(2,1)S(1)} async-done(((bf16[32,2,16,896]{3,2,1,0:T(8,128)(2,1)}), bf16[32,2,16,896]{3,2,1,0:T(8,128)(2,1)S(1)}, u32[]{:S(2)}, u32[]{:S(2)}) %all-to-all-start) | async-done | bytes 1835040 | tf_op jit(solution)/shard_map/all_to_all | solution.py:273
  60.3 1.3 pick.1.a_ref
  61.8 1.4 collective-permute-start.5
  63.6 1.3 collective-permute-start.9
  64.9 5.5 %collective-permute-done.5.a_ref = bf16[256,896]{1,0:T(8,128)(2,1)S(1)} collective-permute-done((bf16[256,896]{1,0:T(8,128)(2,1)S(1)}, bf16[256,896]{1,0:T(8,128)(2,1)S(1)}, u32[]{:S(2)}, u32[]{:S(2)}) %collective-permute-start.5) | collective-permute-done | bytes 458784 | tf_op jit(solution)/shard_map/ppermute | solution.py:297
  70.3 1.8 %collective-permute-start.6 = (bf16[256,896]{1,0:T(8,128)(2,1)S(1)}, bf16[256,896]{1,0:T(8,128)(2,1)S(1)}, u32[]{:S(2)}, u32[]{:S(2)}) collective-permute-start(bf16[256,896]{1,0:T(8,128)(2,1)S(1)} %collective-permute-done.5.a_ref), channel_id=1, source_target_pairs={{0,2},{1,7},{2,4},{3,1},{4,6},{5,3},{6,0},{7,5},{8,10},{9,15},{10,... | collective-permute-start | bytes 1376264 | tf_op jit(solution)/shard_map/ppermute | solution.py:297
  73.0 2.3 %collective-permute-done.9.a_ref = bf16[256,896]{1,0:T(8,128)(2,1)S(1)} collective-permute-done((bf16[256,896]{1,0:T(8,128)(2,1)S(1)}, bf16[256,896]{1,0:T(8,128)(2,1)S(1)}, u32[]{:S(2)}, u32[]{:S(2)}) %collective-permute-start.9) | collective-permute-done | bytes 458784 | tf_op jit(solution)/shard_map/ppermute | solution.py:297
  76.1 4.0 %collective-permute-done.6.refs_6_ = bf16[256,896]{1,0:T(8,128)(2,1)S(1)} collective-permute-done((bf16[256,896]{1,0:T(8,128)(2,1)S(1)}, bf16[256,896]{1,0:T(8,128)(2,1)S(1)}, u32[]{:S(2)}, u32[]{:S(2)}) %collective-permute-start.6) | collective-permute-done | bytes 458784 | tf_op jit(solution)/shard_map/ppermute | solution.py:297
  82.0 9.0 %attend.1 = (bf16[8,64,256]{2,1,0:T(8,128)(2,1)S(1)}, bf16[16,16,896]{2,1,0:T(8,128)(2,1)S(1)}, bf16[16,16,896]{2,1,0:T(8,128)(2,1)S(1)}, f32[1,896]{1,0:T(1,128)S(1)}) custom-call(s32[2]{0:T(128)S(1)} %pad_add_fusion.me_ref, s32[8]{0:T(128)S(1)} %copy-done.6, bf16[8,64,896]{2,1,0:T(8,128)(2,1)S(1)} %get-tuple-element.28.refs_0_, ...), custom_call_target="tpu_custom_call" | custom-call | flops 4200000000 | bytes 8000000 | tf_op jit(solution)/shard_map/attend/pallas_call | solution.py:137
  91.0 1.4 collective-permute-start.19
  92.4 1.2 collective-permute-done.20
  93.5 1.4 collective-permute-start.21
  94.9 2.2 %collective-permute-done.21 = f32[1,896]{1,0:T(1,128)S(1)} collective-permute-done((f32[1,896]{1,0:T(1,128)S(1)}, f32[1,896]{1,0:T(1,128)S(1)}, u32[]{:S(2)}, u32[]{:S(2)}) %collective-permute-start.21) | collective-permute-done | bytes 3616 | tf_op jit(solution)/shard_map/ppermute | solution.py:318
  97.1 1.5 %collective-permute-start.22 = (f32[1,896]{1,0:T(1,128)S(1)}, f32[1,896]{1,0:T(1,128)S(1)}, u32[]{:S(2)}, u32[]{:S(2)}) collective-permute-start(f32[1,896]{1,0:T(1,128)S(1)} %add.108), channel_id=1, source_target_pairs={{0,4},{1,5},{2,6},{3,7},{4,0},{5,1},{6,2},{7,3},{8,12},{9,13},{10,... | collective-permute-start | bytes 10760 | tf_op jit(solution)/shard_map/ppermute | solution.py:318
  98.7 3.6 %collective-permute-done.22 = f32[1,896]{1,0:T(1,128)S(1)} collective-permute-done((f32[1,896]{1,0:T(1,128)S(1)}, f32[1,896]{1,0:T(1,128)S(1)}, u32[]{:S(2)}, u32[]{:S(2)}) %collective-permute-start.22) | collective-permute-done | bytes 3616 | tf_op jit(solution)/shard_map/ppermute | solution.py:318
  103.1 6.0 %all-to-all-start.1 = ((bf16[16,16,896]{2,1,0:T(8,128)(2,1)}), bf16[16,16,896]{2,1,0:T(8,128)(2,1)S(1)}, u32[]{:S(2)}, u32[]{:S(2)}) async-start(bf16[16,16,896]{2,1,0:T(8,128)(2,1)} %pairs.1), calls=%async_computation.1 | async-start | bytes 917504 | tf_op jit(solution)/shard_map/all_to_all | solution.py:347
  109.3 1.6 %collective-permute-start.13 = (bf16[8,8,256]{2,1,0:T(8,128)(2,1)S(1)}, bf16[8,8,256]{2,1,0:T(8,128)(2,1)S(1)}, u32[]{:S(2)}, u32[]{:S(2)}) collective-permute-start(bf16[8,8,256]{2,1,0:T(8,128)(2,1)S(1)} %get-tuple-element.54), channel_id=1, source_target_pairs={{0,2},{1,3},{2,0},{3,1},{4,6},{5,7},{6,4},{7,5},{8,10},{9,11},{10,... | collective-permute-start | bytes 98312 | tf_op jit(solution)/shard_map/ppermute | solution.py:326
  111.2 1.6 %collective-permute-start.15 = (bf16[8,8,256]{2,1,0:T(8,128)(2,1)S(1)}, bf16[8,8,256]{2,1,0:T(8,128)(2,1)S(1)}, u32[]{:S(2)}, u32[]{:S(2)}) collective-permute-start(bf16[8,8,256]{2,1,0:T(8,128)(2,1)S(1)} %get-tuple-element.52), channel_id=1, source_target_pairs={{0,4},{1,5},{2,6},{3,7},{4,0},{5,1},{6,2},{7,3},{8,12},{9,13},{10,... | collective-permute-start | bytes 98312 | tf_op jit(solution)/shard_map/ppermute | solution.py:326
  112.7 1.7 %collective-permute-start.16 = (bf16[8,8,256]{2,1,0:T(8,128)(2,1)S(1)}, bf16[8,8,256]{2,1,0:T(8,128)(2,1)S(1)}, u32[]{:S(2)}, u32[]{:S(2)}) collective-permute-start(bf16[8,8,256]{2,1,0:T(8,128)(2,1)S(1)} %get-tuple-element.51), channel_id=1, source_target_pairs={{0,5},{1,4},{2,7},{3,6},{4,1},{5,0},{6,3},{7,2},{8,13},{9,12},{10,... | collective-permute-start | bytes 98312 | tf_op jit(solution)/shard_map/ppermute | solution.py:326
  115.0 1.4 collective-permute-start.18
  116.6 6.3 %all-to-all-done.1.in_ref = bf16[16,16,896]{2,1,0:T(8,128)(2,1)S(1)} async-done(((bf16[16,16,896]{2,1,0:T(8,128)(2,1)}), bf16[16,16,896]{2,1,0:T(8,128)(2,1)S(1)}, u32[]{:S(2)}, u32[]{:S(2)}) %all-to-all-start.1) | async-done | bytes 458784 | tf_op jit(solution)/shard_map/all_to_all | solution.py:347
  122.9 1.4 reduce.1
  124.3 8.6 %all-to-all-start.2 = ((f32[256,1,128]{2,1,0:T(1,128)}), f32[256,1,128]{2,1,0:T(1,128)S(1)}, u32[]{:S(2)}, u32[]{:S(2)}) async-start(f32[256,1,128]{2,1,0:T(1,128)} %get-tuple-element.41), calls=%async_computation.2 | async-start | bytes 262144 | tf_op jit(solution)/shard_map/all_to_all | solution.py:365
  133.0 2.9 %collective-permute-start.23 = (f32[16,896]{1,0:T(8,128)S(1)}, f32[16,896]{1,0:T(8,128)S(1)}, u32[]{:S(2)}, u32[]{:S(2)}) collective-permute-start(f32[16,896]{1,0:T(8,128)S(1)} %get-tuple-element.42), channel_id=1, source_target_pairs={{0,0},{1,16},{2,32},{3,48},{4,64},{5,80},{6,96},{7,112},{8,1},{9,1... | collective-permute-start | bytes 172040 | tf_op jit(solution)/shard_map/ppermute | solution.py:364
  135.9 14.0 %collective-permute-done.23.red_ref = f32[16,896]{1,0:T(8,128)S(1)} collective-permute-done((f32[16,896]{1,0:T(8,128)S(1)}, f32[16,896]{1,0:T(8,128)S(1)}, u32[]{:S(2)}, u32[]{:S(2)}) %collective-permute-start.23) | collective-permute-done | bytes 57376 | tf_op jit(solution)/shard_map/ppermute | solution.py:364
  (82 shorter events, 12.3 us)
Async XLA Ops:
  5.1 11.4 %copy-start.7 = (bf16[512,896]{1,0:T(8,128)(2,1)S(1)}, bf16[512,896]{1,0:T(8,128)(2,1)}, u32[]{:S(2)}) copy-start(bf16[512,896]{1,0:T(8,128)(2,1)} %param.11) | copy-start | bytes 2752516
  5.1 55.3 %all-to-all-start = ((bf16[32,2,16,896]{3,2,1,0:T(8,128)(2,1)}), bf16[32,2,16,896]{3,2,1,0:T(8,128)(2,1)S(1)}, u32[]{:S(2)}, u32[]{:S(2)}) async-start(bf16[32,2,16,896]{3,2,1,0:T(8,128)(2,1)} %bitcast.30), calls=%async_computation | async-start | bytes 3670016 | tf_op jit(solution)/shard_map/all_to_all | solution.py:273
  17.5 18.9 %collective-permute-start = (bf16[256,896]{1,0:T(8,128)(2,1)}, bf16[256,896]{1,0:T(8,128)(2,1)S(1)}, u32[]{:S(2)}, u32[]{:S(2)}) collective-permute-start(bf16[256,896]{1,0:T(8,128)(2,1)} %get-tuple-element.47), channel_id=1, source_target_pairs={{0,1},{1,3},{2,5},{3,7},{4,0},{5,2},{6,4},{7,6},{8,9},{9,11},{10,1... | collective-permute-start | bytes 1376264 | tf_op jit(solution)/shard_map/ppermute | solution.py:286
  17.8 18.6 %collective-permute-start.1 = (bf16[256,896]{1,0:T(8,128)(2,1)}, bf16[256,896]{1,0:T(8,128)(2,1)S(1)}, u32[]{:S(2)}, u32[]{:S(2)}) collective-permute-start(bf16[256,896]{1,0:T(8,128)(2,1)} %get-tuple-element.48), channel_id=1, source_target_pairs={{0,0},{1,2},{2,4},{3,6},{4,1},{5,3},{6,5},{7,7},{8,8},{9,10},{10,1... | collective-permute-start | bytes 1376264 | tf_op jit(solution)/shard_map/ppermute | solution.py:285
  20.0 1.9 %collective-permute-start.2 = (bf16[1,896]{1,0:T(2,128)(2,1)S(1)}, bf16[1,896]{1,0:T(2,128)(2,1)S(1)}, u32[]{:S(2)}, u32[]{:S(2)}) collective-permute-start(bf16[1,896]{1,0:T(2,128)(2,1)S(1)} %compare_select_fusion), channel_id=1, source_target_pairs={{0,1},{1,0},{2,3},{3,2},{4,5},{5,4},{6,7},{7,6},{8,9},{9,8},{10,11... | collective-permute-start | bytes 5384 | tf_op jit(solution)/shard_map/ppermute | solution.py:292
  21.9 9.2 %collective-permute-start.3 = (bf16[1,896]{1,0:T(2,128)(2,1)S(1)}, bf16[1,896]{1,0:T(2,128)(2,1)S(1)}, u32[]{:S(2)}, u32[]{:S(2)}) collective-permute-start(bf16[1,896]{1,0:T(2,128)(2,1)S(1)} %fusion.2), channel_id=1, source_target_pairs={{0,2},{1,3},{2,0},{3,1},{4,6},{5,7},{6,4},{7,5},{8,10},{9,11},{10,... | collective-permute-start | bytes 5384 | tf_op jit(solution)/shard_map/ppermute | solution.py:292
  31.2 5.2 %collective-permute-start.4 = (bf16[1,896]{1,0:T(2,128)(2,1)S(1)}, bf16[1,896]{1,0:T(2,128)(2,1)S(1)}, u32[]{:S(2)}, u32[]{:S(2)}) collective-permute-start(bf16[1,896]{1,0:T(2,128)(2,1)S(1)} %add.89), channel_id=1, source_target_pairs={{0,4},{1,5},{2,6},{3,7},{4,0},{5,1},{6,2},{7,3},{8,12},{9,13},{10,... | collective-permute-start | bytes 5384 | tf_op jit(solution)/shard_map/ppermute | solution.py:292
  61.7 1.9 %collective-permute-start.7 = (bf16[256,896]{1,0:T(8,128)(2,1)S(1)}, bf16[256,896]{1,0:T(8,128)(2,1)S(1)}, u32[]{:S(2)}, u32[]{:S(2)}) collective-permute-start(bf16[256,896]{1,0:T(8,128)(2,1)S(1)} %pick.1.a_ref), channel_id=1, source_target_pairs={{0,1},{1,0},{2,3},{3,2},{4,5},{5,4},{6,7},{7,6},{8,9},{9,8},{10,11... | collective-permute-start | bytes 1376264 | tf_op jit(solution)/shard_map/ppermute | solution.py:297
  61.8 8.6 %collective-permute-start.5 = (bf16[256,896]{1,0:T(8,128)(2,1)S(1)}, bf16[256,896]{1,0:T(8,128)(2,1)S(1)}, u32[]{:S(2)}, u32[]{:S(2)}) collective-permute-start(bf16[256,896]{1,0:T(8,128)(2,1)S(1)} %pick.1.a_ref), channel_id=1, source_target_pairs={{0,2},{1,7},{2,4},{3,1},{4,6},{5,3},{6,0},{7,5},{8,10},{9,15},{10,... | collective-permute-start | bytes 1376264 | tf_op jit(solution)/shard_map/ppermute | solution.py:297
  63.6 11.7 %collective-permute-start.9 = (bf16[256,896]{1,0:T(8,128)(2,1)S(1)}, bf16[256,896]{1,0:T(8,128)(2,1)S(1)}, u32[]{:S(2)}, u32[]{:S(2)}) collective-permute-start(bf16[256,896]{1,0:T(8,128)(2,1)S(1)} %collective-permute-done.7.b_ref), channel_id=1, source_target_pairs={{0,2},{1,7},{2,4},{3,1},{4,6},{5,3},{6,0},{7,5},{8,10},{9,15},{10,... | collective-permute-start | bytes 1376264 | tf_op jit(solution)/shard_map/ppermute | solution.py:297
  70.3 4.9 %collective-permute-start.8 = (bf16[256,896]{1,0:T(8,128)(2,1)S(1)}, bf16[256,896]{1,0:T(8,128)(2,1)S(1)}, u32[]{:S(2)}, u32[]{:S(2)}) collective-permute-start(bf16[256,896]{1,0:T(8,128)(2,1)S(1)} %collective-permute-done.5.a_ref), channel_id=1, source_target_pairs={{0,1},{1,0},{2,3},{3,2},{4,5},{5,4},{6,7},{7,6},{8,9},{9,8},{10,11... | collective-permute-start | bytes 1376264 | tf_op jit(solution)/shard_map/ppermute | solution.py:297
  70.3 9.8 %collective-permute-start.6 = (bf16[256,896]{1,0:T(8,128)(2,1)S(1)}, bf16[256,896]{1,0:T(8,128)(2,1)S(1)}, u32[]{:S(2)}, u32[]{:S(2)}) collective-permute-start(bf16[256,896]{1,0:T(8,128)(2,1)S(1)} %collective-permute-done.5.a_ref), channel_id=1, source_target_pairs={{0,2},{1,7},{2,4},{3,1},{4,6},{5,3},{6,0},{7,5},{8,10},{9,15},{10,... | collective-permute-start | bytes 1376264 | tf_op jit(solution)/shard_map/ppermute | solution.py:297
  72.1 9.9 %copy-start.5 = (bf16[8,64,2048]{2,1,0:T(8,128)(2,1)S(1)}, bf16[8,64,2048]{2,1,0:T(8,128)(2,1)}, u32[]{:S(2)}) copy-start(bf16[8,64,2048]{2,1,0:T(8,128)(2,1)} %refs_11_.1) | copy-start | bytes 6291460
  73.0 9.0 %copy-start.4 = (bf16[8,64,2048]{2,1,0:T(8,128)(2,1)S(1)}, bf16[8,64,2048]{2,1,0:T(8,128)(2,1)}, u32[]{:S(2)}) copy-start(bf16[8,64,2048]{2,1,0:T(8,128)(2,1)} %refs_10_.1) | copy-start | bytes 6291460
  73.0 9.0 %copy-start.6 = (s32[8]{0:T(128)S(1)}, s32[8]{0:T(128)}, u32[]{:S(2)}) copy-start(s32[8]{0:T(128)} %count_ref.1) | copy-start | bytes 100
  75.2 4.9 %collective-permute-start.10 = (bf16[256,896]{1,0:T(8,128)(2,1)S(1)}, bf16[256,896]{1,0:T(8,128)(2,1)S(1)}, u32[]{:S(2)}, u32[]{:S(2)}) collective-permute-start(bf16[256,896]{1,0:T(8,128)(2,1)S(1)} %collective-permute-done.9.a_ref), channel_id=1, source_target_pairs={{0,1},{1,0},{2,3},{3,2},{4,5},{5,4},{6,7},{7,6},{8,9},{9,8},{10,11... | collective-permute-start | bytes 1376264 | tf_op jit(solution)/shard_map/ppermute | solution.py:297
  80.2 1.8 %collective-permute-start.11 = (bf16[256,896]{1,0:T(8,128)(2,1)S(1)}, bf16[256,896]{1,0:T(8,128)(2,1)S(1)}, u32[]{:S(2)}, u32[]{:S(2)}) collective-permute-start(bf16[256,896]{1,0:T(8,128)(2,1)S(1)} %collective-permute-done.6.refs_6_), channel_id=1, source_target_pairs={{0,1},{1,0},{2,3},{3,2},{4,5},{5,4},{6,7},{7,6},{8,9},{9,8},{10,11... | collective-permute-start | bytes 1376264 | tf_op jit(solution)/shard_map/ppermute | solution.py:297
  91.0 11.3 %collective-permute-start.19 = (bf16[16,16,896]{2,1,0:T(8,128)(2,1)S(1)}, bf16[16,16,896]{2,1,0:T(8,128)(2,1)S(1)}, u32[]{:S(2)}, u32[]{:S(2)}) collective-permute-start(bf16[16,16,896]{2,1,0:T(8,128)(2,1)S(1)} %get-tuple-element.37), channel_id=1, source_target_pairs={{0,64},{1,193},{2,66},{3,195},{4,68},{5,197},{6,70},{7,199},{8,72}... | collective-permute-start | bytes 1376264 | tf_op jit(solution)/shard_map/ppermute | solution.py:336
  92.4 1.2 collective-permute-start.20
  93.5 3.6 %collective-permute-start.21 = (f32[1,896]{1,0:T(1,128)S(1)}, f32[1,896]{1,0:T(1,128)S(1)}, u32[]{:S(2)}, u32[]{:S(2)}) collective-permute-start(f32[1,896]{1,0:T(1,128)S(1)} %add.107), channel_id=1, source_target_pairs={{0,2},{1,3},{2,0},{3,1},{4,6},{5,7},{6,4},{7,5},{8,10},{9,11},{10,... | collective-permute-start | bytes 10760 | tf_op jit(solution)/shard_map/ppermute | solution.py:318
  97.1 5.1 %collective-permute-start.22 = (f32[1,896]{1,0:T(1,128)S(1)}, f32[1,896]{1,0:T(1,128)S(1)}, u32[]{:S(2)}, u32[]{:S(2)}) collective-permute-start(f32[1,896]{1,0:T(1,128)S(1)} %add.108), channel_id=1, source_target_pairs={{0,4},{1,5},{2,6},{3,7},{4,0},{5,1},{6,2},{7,3},{8,12},{9,13},{10,... | collective-permute-start | bytes 10760 | tf_op jit(solution)/shard_map/ppermute | solution.py:318
  103.1 19.8 %all-to-all-start.1 = ((bf16[16,16,896]{2,1,0:T(8,128)(2,1)}), bf16[16,16,896]{2,1,0:T(8,128)(2,1)S(1)}, u32[]{:S(2)}, u32[]{:S(2)}) async-start(bf16[16,16,896]{2,1,0:T(8,128)(2,1)} %pairs.1), calls=%async_computation.1 | async-start | bytes 917504 | tf_op jit(solution)/shard_map/all_to_all | solution.py:347
  109.2 5.2 %collective-permute-start.12 = (bf16[8,8,256]{2,1,0:T(8,128)(2,1)S(1)}, bf16[8,8,256]{2,1,0:T(8,128)(2,1)S(1)}, u32[]{:S(2)}, u32[]{:S(2)}) collective-permute-start(bf16[8,8,256]{2,1,0:T(8,128)(2,1)S(1)} %get-tuple-element.55), channel_id=1, source_target_pairs={{0,1},{1,0},{2,3},{3,2},{4,5},{5,4},{6,7},{7,6},{8,9},{9,8},{10,11... | collective-permute-start | bytes 98312 | tf_op jit(solution)/shard_map/ppermute | solution.py:326
  109.3 5.7 %collective-permute-start.13 = (bf16[8,8,256]{2,1,0:T(8,128)(2,1)S(1)}, bf16[8,8,256]{2,1,0:T(8,128)(2,1)S(1)}, u32[]{:S(2)}, u32[]{:S(2)}) collective-permute-start(bf16[8,8,256]{2,1,0:T(8,128)(2,1)S(1)} %get-tuple-element.54), channel_id=1, source_target_pairs={{0,2},{1,3},{2,0},{3,1},{4,6},{5,7},{6,4},{7,5},{8,10},{9,11},{10,... | collective-permute-start | bytes 98312 | tf_op jit(solution)/shard_map/ppermute | solution.py:326
  110.9 5.5 %collective-permute-start.14 = (bf16[8,8,256]{2,1,0:T(8,128)(2,1)S(1)}, bf16[8,8,256]{2,1,0:T(8,128)(2,1)S(1)}, u32[]{:S(2)}, u32[]{:S(2)}) collective-permute-start(bf16[8,8,256]{2,1,0:T(8,128)(2,1)S(1)} %get-tuple-element.53), channel_id=1, source_target_pairs={{0,3},{1,2},{2,1},{3,0},{4,7},{5,6},{6,5},{7,4},{8,11},{9,10},{10,... | collective-permute-start | bytes 98312 | tf_op jit(solution)/shard_map/ppermute | solution.py:326
  111.2 5.4 %collective-permute-start.15 = (bf16[8,8,256]{2,1,0:T(8,128)(2,1)S(1)}, bf16[8,8,256]{2,1,0:T(8,128)(2,1)S(1)}, u32[]{:S(2)}, u32[]{:S(2)}) collective-permute-start(bf16[8,8,256]{2,1,0:T(8,128)(2,1)S(1)} %get-tuple-element.52), channel_id=1, source_target_pairs={{0,4},{1,5},{2,6},{3,7},{4,0},{5,1},{6,2},{7,3},{8,12},{9,13},{10,... | collective-permute-start | bytes 98312 | tf_op jit(solution)/shard_map/ppermute | solution.py:326
  112.7 20.2 %collective-permute-start.16 = (bf16[8,8,256]{2,1,0:T(8,128)(2,1)S(1)}, bf16[8,8,256]{2,1,0:T(8,128)(2,1)S(1)}, u32[]{:S(2)}, u32[]{:S(2)}) collective-permute-start(bf16[8,8,256]{2,1,0:T(8,128)(2,1)S(1)} %get-tuple-element.51), channel_id=1, source_target_pairs={{0,5},{1,4},{2,7},{3,6},{4,1},{5,0},{6,3},{7,2},{8,13},{9,12},{10,... | collective-permute-start | bytes 98312 | tf_op jit(solution)/shard_map/ppermute | solution.py:326
  114.5 18.5 %collective-permute-start.17 = (bf16[8,8,256]{2,1,0:T(8,128)(2,1)S(1)}, bf16[8,8,256]{2,1,0:T(8,128)(2,1)S(1)}, u32[]{:S(2)}, u32[]{:S(2)}) collective-permute-start(bf16[8,8,256]{2,1,0:T(8,128)(2,1)S(1)} %get-tuple-element.50), channel_id=1, source_target_pairs={{0,6},{1,7},{2,4},{3,5},{4,2},{5,3},{6,0},{7,1},{8,14},{9,15},{10,... | collective-permute-start | bytes 98312 | tf_op jit(solution)/shard_map/ppermute | solution.py:326
  115.0 20.9 %collective-permute-start.18 = (bf16[8,8,256]{2,1,0:T(8,128)(2,1)S(1)}, bf16[8,8,256]{2,1,0:T(8,128)(2,1)S(1)}, u32[]{:S(2)}, u32[]{:S(2)}) collective-permute-start(bf16[8,8,256]{2,1,0:T(8,128)(2,1)S(1)} %get-tuple-element.49), channel_id=1, source_target_pairs={{0,7},{1,6},{2,5},{3,4},{4,3},{5,2},{6,1},{7,0},{8,15},{9,14},{10,... | collective-permute-start | bytes 98312 | tf_op jit(solution)/shard_map/ppermute | solution.py:326
  124.3 25.6 %all-to-all-start.2 = ((f32[256,1,128]{2,1,0:T(1,128)}), f32[256,1,128]{2,1,0:T(1,128)S(1)}, u32[]{:S(2)}, u32[]{:S(2)}) async-start(f32[256,1,128]{2,1,0:T(1,128)} %get-tuple-element.41), calls=%async_computation.2 | async-start | bytes 262144 | tf_op jit(solution)/shard_map/all_to_all | solution.py:365
  133.0 16.9 %collective-permute-start.23 = (f32[16,896]{1,0:T(8,128)S(1)}, f32[16,896]{1,0:T(8,128)S(1)}, u32[]{:S(2)}, u32[]{:S(2)}) collective-permute-start(f32[16,896]{1,0:T(8,128)S(1)} %get-tuple-element.42), channel_id=1, source_target_pairs={{0,0},{1,16},{2,32},{3,48},{4,64},{5,80},{6,96},{7,112},{8,1},{9,1... | collective-permute-start | bytes 172040 | tf_op jit(solution)/shard_map/ppermute | solution.py:364
  135.9 15.0 %copy-start.8 = (bf16[8,8,2048]{2,1,0:T(8,128)(2,1)}, bf16[8,8,2048]{2,1,0:T(8,128)(2,1)S(1)}, u32[]{:S(2)}) copy-start(bf16[8,8,2048]{2,1,0:T(8,128)(2,1)S(1)} %constant_dynamic-update-slice_fusion) | copy-start | bytes 786436
  (5 other events, 12.0 us)
